TPU v7x, 768 devices: a whole 4x8x12 slice. The times are simulated.
768 devices in a mesh: box: 64 (over x, y, core), grp: 12 (over z).
Axes of the slice: x: 4, y: 8, z: 12, core: 2. Of those that a mesh axis runs over, the one named last changes fastest.
Arguments:
- source: bfloat16 [122880, 32, 32], P(('box', 'grp')), may hold values from -6 to 6
- conductivity: bfloat16 [122880, 32, 32], P(('box', 'grp')), may hold values from 0.25 to 4
- new_owner: int32 [64, 12, 5, 1], P('box', 'grp'), may hold values from 0 to 11; in each aligned block of 5 rows (0 to 4, 5 to 9, ..., all dimensions but the last counted through in order) at most 2 rows name the same one
Outputs:
- correction: bfloat16 [64, 12, 12, 2, 32768], P('box', 'grp')
- coarse_residual: float32 [12, 320, 4096], P('grp')
Inputs may be any that keep to these rules, and one draw needn't show every extreme that they name: `new_owner`: boxes move only within their box index; among the 5 boxes of one device at most 2 share a new owner, and in every draw some device gives exactly 2 boxes to one owner.
All inputs are finite; a program needn't handle non-finite values.
Results may differ from a plain program's by a relative error of at most 0.001.
Values may be sent and summed in bfloat16 or wider, within the bound.
No kernel may reach another device: no remote copies, remote signals or barrier semaphores. Data moves between devices by JAX's collectives and lax.ppermute only.
A program may use at most 128 MiB of HBM per device.

v0:
```python
import jax
import jax.numpy as jnp
from jax import lax
from jax.sharding import PartitionSpec as P

WEIGHT = 0.8


def padded_2(cells, sides, width):
    for axis, dim in sides:
        count = lax.axis_size(axis)
        ends = count - 1
        head = lax.slice_in_dim(cells, 0, width, axis=dim)
        tail = lax.slice_in_dim(cells, cells.shape[dim] - width, cells.shape[dim], axis=dim)
        cells = jnp.concatenate(
            [
                lax.ppermute(tail, axis, [(i, (i + 1) % count) for i in range(ends)]),
                cells,
                lax.ppermute(head, axis, [((i + 1) % count, i) for i in range(ends)]),
            ],
            axis=dim,
        )
    return cells


def shift_next(values_in, which):
    extent = values_in.shape[which]
    widths = [(0, 0)] * values_in.ndim
    widths[which] = (0, 1)
    return jnp.pad(lax.slice_in_dim(values_in, 1, extent, axis=which), widths)


def shift_prev(values_in, which):
    extent = values_in.shape[which]
    widths = [(0, 0)] * values_in.ndim
    widths[which] = (1, 0)
    return jnp.pad(lax.slice_in_dim(values_in, 0, extent - 1, axis=which), widths)


def smooth(source, conductivity):
    inside = conductivity > 0
    axes_list = (conductivity.ndim - 3, conductivity.ndim - 2, conductivity.ndim - 1)
    face_list = []
    diagonal = jnp.zeros_like(conductivity)
    for which in axes_list:
        after = shift_next(conductivity, which)
        face_fwd = jnp.where(inside & (after > 0), 0.5 * (conductivity + after), 0.0)
        face_list.append(face_fwd)
        before = shift_prev(conductivity, which)
        face_bwd = shift_prev(face_fwd, which)
        diagonal = diagonal + jnp.where(after > 0, face_fwd, conductivity)
        diagonal = diagonal + jnp.where(before > 0, face_bwd, conductivity)
    divisor = jnp.where(inside, diagonal, 1.0)

    def operate(values_in):
        result = diagonal * values_in
        for which, face_fwd in zip(axes_list, face_list):
            result = result - face_fwd * shift_next(values_in, which)
            result = result - shift_prev(face_fwd * values_in, which)
        return result

    sweep_one = jnp.where(inside, WEIGHT * source / divisor, 0.0)
    sweep_two = jnp.where(inside, sweep_one + WEIGHT * (source - operate(sweep_one)) / divisor, 0.0)
    leftover = jnp.where(inside, source - operate(sweep_two), 0.0)
    return (sweep_two, leftover)


def restrict(leftover):
    leading = leftover.shape[:-3]
    layers, rows_y, rows_x = leftover.shape[-3:]
    blocks = leftover.reshape(leading + (layers // 2, 2, rows_y // 2, 2, rows_x // 2, 2))
    return jnp.mean(blocks, axis=(-5, -3, -1)).reshape(leading + (-1,))


def ranks_of(owners):
    count = owners.shape[-1]
    order = jnp.arange(count)
    earlier = (owners[..., :, None] == owners[..., None, :]) & (order[:, None] < order[None, :])
    return jnp.sum(earlier.astype(jnp.int32), axis=-2)


def shards(source, conductivity, new_owner):
    total_layers, rows_y, rows_x = source.shape
    box_count = new_owner.shape[2]
    layers = total_layers // box_count
    box_cells = layers * rows_y * rows_x
    group_count = lax.axis_size("grp")
    slots_per = max(2, (2 * box_count + group_count - 1) // group_count)
    stacked = jnp.stack([source, conductivity])
    padded = padded_2(stacked, ((("box", "grp"), 1),), 3)
    sweep_two, leftover = smooth(padded[0].astype(jnp.float32), padded[1].astype(jnp.float32))
    settled = sweep_two[3 : 3 + total_layers].reshape(box_count, box_cells).astype(jnp.bfloat16)
    restricted = restrict(leftover[3 : 3 + total_layers].reshape(box_count, layers, rows_y, rows_x))
    owners = new_owner.reshape(box_count)
    gathered, owner_list = (
        lax.all_gather(settled, "grp", axis=0, tiled=True),
        lax.all_gather(owners.astype(jnp.bfloat16), "grp", axis=0, tiled=True),
    )
    owner_ids = owner_list.astype(jnp.int32).reshape(group_count, box_count)
    rank_all = ranks_of(owner_ids)
    mine = owner_ids == lax.axis_index("grp")
    slot_ids = jnp.arange(slots_per, dtype=jnp.int32)
    select = (mine[:, :, None] & (rank_all[:, :, None] == slot_ids[None, None, :])).astype(
        jnp.bfloat16
    )
    boxes = gathered.reshape(group_count, box_count, box_cells)
    received = jnp.einsum("gkr,gkc->grc", select, boxes, preferred_element_type=jnp.float32).astype(
        jnp.bfloat16
    )
    coarse = lax.all_gather(restricted, "box", axis=0, tiled=True)
    return (
        received.reshape(1, 1, group_count, slots_per, box_cells),
        coarse.reshape(1, coarse.shape[0], coarse.shape[1]),
    )


def solution(mesh):
    placed = (
        P(("box", "grp"), None, None),
        P(("box", "grp"), None, None),
        P("box", "grp", None, None),
    )
    return jax.shard_map(
        shards,
        mesh=mesh,
        in_specs=placed,
        out_specs=(P("box", "grp", None, None, None), P("grp", None, None)),
        check_vma=False,
    )
```

profile of v0, /device:TPU:56, one launch (start us, length us, event | category | flops | bytes accessed | tf_op | source)
XLA Modules:
  0.0 244.4 jit_solution(10566405423428082073)
XLA Ops:
  7.2 1.5 fusion.3
  8.7 4.3 %collective-permute-start = (bf16[2,3,32,32]{1,3,2,0:T(8,128)(2,1)S(1)}, bf16[2,3,32,32]{1,3,2,0:T(8,128)(2,1)S(1)}, u32[]{:S(2)}, u32[]{:S(2)}) collective-permute-start(bf16[2,3,32,32]{1,3,2,0:T(8,128)(2,1)S(1)} %get-tuple-element.29), channel_id=1, source_target_pairs={{0,1},{1,2},{2,3},{3,4},{4,5},{5,6},{6,7},{7,8},{8,9},{9,10},{10,1... | collective-permute-start | bytes 36872 | tf_op jit(solution)/shard_map/ppermute | solution.py:17
  13.0 12.5 %collective-permute-start.1 = (bf16[2,3,32,32]{1,3,2,0:T(8,128)(2,1)S(1)}, bf16[2,3,32,32]{1,3,2,0:T(8,128)(2,1)S(1)}, u32[]{:S(2)}, u32[]{:S(2)}) collective-permute-start(bf16[2,3,32,32]{1,3,2,0:T(8,128)(2,1)S(1)} %get-tuple-element.30), channel_id=1, source_target_pairs={{1,0},{2,1},{3,2},{4,3},{5,4},{6,5},{7,6},{8,7},{9,8},{10,9},{11,1... | collective-permute-start | bytes 36872 | tf_op jit(solution)/shard_map/ppermute | solution.py:19
  25.5 9.7 %collective-permute-done = bf16[2,3,32,32]{1,3,2,0:T(8,128)(2,1)S(1)} collective-permute-done((bf16[2,3,32,32]{1,3,2,0:T(8,128)(2,1)S(1)}, bf16[2,3,32,32]{1,3,2,0:T(8,128)(2,1)S(1)}, u32[]{:S(2)}, u32[]{:S(2)}) %collective-permute-start) | collective-permute-done | bytes 12320 | tf_op jit(solution)/shard_map/ppermute | solution.py:17
  35.2 1.8 collective-permute-done.1
  37.7 1.2 fusion.4
  40.9 1.8 divide_select_fusion
  43.7 1.5 add_select_fusion
  45.2 1.0 slice.204
  46.2 2.8 %copy.17 = bf16[160,32,32]{2,1,0:T(8,128)(2,1)} copy(bf16[160,32,32]{0,2,1:T(8,128)(2,1)} %slice.204) | data formatting | bytes 655360 | tf_op jit(solution)/shard_map/slice | solution.py:92
  49.0 3.4 %reshape.67 = bf16[1,5,32768]{2,1,0:T(8,128)(2,1)} reshape(bf16[160,32,32]{2,1,0:T(8,128)(2,1)} %copy.17) | data formatting | bytes 655360
  52.6 1.4 fusion.12
  54.7 0.9 copy-done.1
  56.0 0.9 pad_multiply_fusion.1
  57.2 2.3 fusion.1
  59.5 23.9 %reshape_reshape.3 = f32[5,16,2,16,2,16,2]{2,1,0,6,5,4,3:T(8,128)} reshape(f32[160,32,32]{0,2,1:T(8,128)S(1)} %fusion.1) | data formatting | bytes 1310720 | tf_op jit(solution)/shard_map/reshape;reshape | solution.py:71
  83.4 15.5 %reduce_sum.19 = f32[5,16,16,16]{1,0,3,2:T(8,128)S(1)} reduce(f32[5,16,2,16,2,16,2]{2,1,0,6,5,4,3:T(8,128)} %reshape_reshape.3, f32[]{:T(128)} %constant.2.clone.1), dimensions={2,4,6}, to_apply=%region_1.2 | reduce | flops 143360 | bytes 737284 | tf_op jit(solution)/shard_map/reduce_sum | solution.py:72
  99.4 1.0 reshape.69
  100.4 1.3 dynamic-slice
  102.6 23.8 %all-reduce.21 = bf16[60]{0:T(256)(128)(2,1)S(1)} all-reduce(bf16[60]{0:T(256)(128)(2,1)S(1)} %dynamic-update-slice), channel_id=2, replica_groups=mesh['box'=64,'grp'=12] {'grp'}, use_global_device_ids=true, to_apply=%add.21 | all-reduce | flops 60 | bytes 240
  126.8 8.5 %all-gather.6.cloned.1.call-done = bf16[12,5,32768]{2,1,0:T(8,128)(2,1)} async-done(((bf16[1,5,32768]{2,1,0:T(8,128)(2,1)}), bf16[12,5,32768]{2,1,0:T(8,128)(2,1)}) %all-gather.6.cloned.1.call-update) | async-done | bytes 3932176 | tf_op jit(solution)/shard_map/all_gather | solution.py:96
  135.3 5.7 %fusion = bf16[1,1,12,2,32768]{4,3,2,1,0:T(2,128)(2,1)} fusion(bf16[12,5,32768]{2,1,0:T(8,128)(2,1)} %all-gather.6.cloned.1.call-done, pred[12,5]{1,0:T(8,128)(4,1)S(1)} %broadcast_compare_fusion.1, s32[12,5]{1,0:T(8,128)S(1)} %copy.16), kind=kOutput, calls=%fused_computation.1 | convolution fusion | flops 8650992 | bytes 5505324 | tf_op jit(solution)/shard_map/gkr,gkc->grc/dot_general | solution.py:107
  141.0 90.3 %all-gather.8.cloned.1.call-done = f32[64,5,4096]{2,1,0:T(8,128)} async-done(((f32[1,5,4096]{2,1,0:T(8,128)}), f32[64,5,4096]{2,1,0:T(8,128)}) %all-gather.8.cloned.1.call-update) | async-done | bytes 5242896 | tf_op jit(solution)/shard_map/all_gather | solution.py:110
  231.3 6.3 %reshape.56 = f32[1,320,4096]{2,1,0:T(8,128)} reshape(f32[64,5,4096]{2,1,0:T(8,128)} %all-gather.8.cloned.1.call-done) | data formatting | bytes 10485760 | tf_op jit(solution)/shard_map/reshape | solution.py:113
  (43 shorter events, 6.3 us)
Async XLA Ops:
  7.2 29.8 %copy-start.5 = (bf16[160,32,32]{0,2,1:T(8,128)(2,1)S(1)}, bf16[160,32,32]{0,2,1:T(8,128)(2,1)}, u32[]{:S(2)}) copy-start(bf16[160,32,32]{0,2,1:T(8,128)(2,1)} %param.3) | copy-start | bytes 983044
  7.2 29.8 %copy-start.6 = (bf16[160,32,32]{0,2,1:T(8,128)(2,1)S(1)}, bf16[160,32,32]{0,2,1:T(8,128)(2,1)}, u32[]{:S(2)}) copy-start(bf16[160,32,32]{0,2,1:T(8,128)(2,1)} %param.4) | copy-start | bytes 983044
  7.2 128.1 %all-gather.6.cloned.1.call-start = ((), (), s32[]{:S(2)}) async-start(), calls=%async_computation | async-start | bytes 6815744 | tf_op jit(solution)/shard_map/all_gather | solution.py:96
  8.7 26.5 %collective-permute-start = (bf16[2,3,32,32]{1,3,2,0:T(8,128)(2,1)S(1)}, bf16[2,3,32,32]{1,3,2,0:T(8,128)(2,1)S(1)}, u32[]{:S(2)}, u32[]{:S(2)}) collective-permute-start(bf16[2,3,32,32]{1,3,2,0:T(8,128)(2,1)S(1)} %get-tuple-element.29), channel_id=1, source_target_pairs={{0,1},{1,2},{2,3},{3,4},{4,5},{5,6},{6,7},{7,8},{8,9},{9,10},{10,1... | collective-permute-start | bytes 36872 | tf_op jit(solution)/shard_map/ppermute | solution.py:17
  13.0 24.0 %collective-permute-start.1 = (bf16[2,3,32,32]{1,3,2,0:T(8,128)(2,1)S(1)}, bf16[2,3,32,32]{1,3,2,0:T(8,128)(2,1)S(1)}, u32[]{:S(2)}, u32[]{:S(2)}) collective-permute-start(bf16[2,3,32,32]{1,3,2,0:T(8,128)(2,1)S(1)} %get-tuple-element.30), channel_id=1, source_target_pairs={{1,0},{2,1},{3,2},{4,3},{5,4},{6,5},{7,6},{8,7},{9,8},{10,9},{11,1... | collective-permute-start | bytes 36872 | tf_op jit(solution)/shard_map/ppermute | solution.py:19
  40.8 2.8 %copy-start = (f32[166,32,32]{0,2,1:T(8,128)}, f32[166,32,32]{0,2,1:T(8,128)S(1)}, u32[]{:S(2)}) copy-start(f32[166,32,32]{0,2,1:T(8,128)S(1)} %get-tuple-element.6) | copy-start | bytes 2039812
  42.6 1.1 copy-start.2
  52.4 178.9 %all-gather.8.cloned.1.call-start = ((), (), s32[]{:S(2)}) async-start(), calls=%async_computation.1 | async-start | bytes 8519680 | tf_op jit(solution)/shard_map/all_gather | solution.py:110
  54.4 1.2 copy-start.1
  54.4 1.5 copy-start.3
  56.0 1.2 copy-start.4
  98.9 3.4 %copy-start.7 = (s32[1,1,5,1]{2,3,1,0:T(1,128)S(1)}, s32[1,1,5,1]{2,3,1,0:T(1,128)}, u32[]{:S(2)}) copy-start(s32[1,1,5,1]{2,3,1,0:T(1,128)} %param.5) | copy-start | bytes 64
Sparse Core Ops, SparseCore 0:
  52.5 82.7 all-gather.5
  139.8 91.4 all-gather.7
where the time goes:
time: 247 us; the launch traced here: 244 us
  waiting for transfers between devices  110 us (45%)
  local copies, waits for them, and re-layouts  43.2 us (17%)
  other arithmetic  29.5 us (12%)
  blocking collectives  23.8 us (10%)
  starting transfers between devices  17 us (7%)
  between operations  14.9 us (6%)
  matrix products  5.7 us (2%)
    all_gather x1, waiting for transfers between devices, shards(): coarse = lax.all_gather(restricted, 'box', axis=0, tiled=True)  90.3 us
    another operation x1, local copies, waits for them, and re-layouts, restrict(): leftover.reshape(leading + (layers // 2, 2, rows_y // 2, 2, rows_x // 2, 2))  23.9 us
    unnamed x1, blocking collectives  23.8 us
    reduce_sum x1, other arithmetic, restrict(): return jnp.mean(blocks, axis=(-5, -3, -1)).reshape(leading + (-1,))  15.5 us
    ppermute x1, starting transfers between devices, padded_2(): lax.ppermute(head, axis, [((i + 1) % count, i) for i in range(ends)])  12.5 us
    ppermute x1, waiting for transfers between devices, padded_2(): lax.ppermute(tail, axis, [(i, (i + 1) % count) for i in range(ends)])  9.71 us
    all_gather x1, waiting for transfers between devices, shards(): lax.all_gather(settled, 'grp', axis=0, tiled=True)  8.54 us
    unnamed x21, local copies, waits for them, and re-layouts  7.62 us
  transfers between devices with their start and end apart: 4, of which 4 were waited for; matrix products, arithmetic and copies ran while one was open for 22% of the time, Pallas kernels for 0%

commit v1 on v0

v1 whole, which is shorter than its diff:
```python
import functools

import jax
import jax.numpy as jnp
from jax import lax
from jax.experimental import pallas as pl
from jax.experimental.pallas import tpu as pltpu
from jax.sharding import Mesh, PartitionSpec as P

WEIGHT = 0.8
F32, BF16, F16 = jnp.float32, jnp.bfloat16, jnp.float16
HALO = 3
EDGE = 4
SUB, LANES = 8, 128
VMEM_LIMIT = 40 * 1024 * 1024


def _iota(shape, dim):
    return lax.broadcasted_iota(jnp.int32, shape, dim)


def _chunks(lo, hi, step, body):
    whole = (hi - lo) // step
    if whole:

        @pl.loop(0, whole)
        def _(i):
            body(lo + i * step, step)

    if lo + whole * step < hi:
        body(lo + whole * step, hi - lo - whole * step)


def _load(ref, layer, count):
    if isinstance(layer, int):
        rows = ref[layer * SUB : (layer + count) * SUB, :]
    else:
        rows = ref[pl.ds(pl.multiple_of(layer * SUB, SUB), count * SUB), :]
    return rows.reshape(count, SUB, LANES)


def _store(ref, layer, value):
    count = value.shape[0]
    rows = value.reshape(count * SUB, LANES)
    if isinstance(layer, int):
        ref[layer * SUB : (layer + count) * SUB, :] = rows
    else:
        ref[pl.ds(pl.multiple_of(layer * SUB, SUB), count * SUB), :] = rows


def _next_x(v):
    return pltpu.roll(v, LANES - 1, 2)


def _prev_x(v):
    return pltpu.roll(v, 1, 2)


def _next_y(v):
    turned = pltpu.roll(v, LANES - 32, 2)
    return jnp.where(_iota(v.shape, 2) < 96, turned, pltpu.roll(turned, SUB - 1, 1))


def _prev_y(v):
    turned = pltpu.roll(v, 32, 2)
    return jnp.where(_iota(v.shape, 2) >= 32, turned, pltpu.roll(turned, 1, 1))


def _transposed(cells_ref, out_ref, layer_of, layers):
    total = cells_ref.shape[1]
    pick = (_iota((layers, total), 1) == layer_of(_iota((layers, total), 0))).astype(BF16)
    for j in range(SUB):
        part = lax.dot_general(
            pick,
            cells_ref[j * LANES : (j + 1) * LANES, :],
            (((1,), (1,)), ((), ())),
            preferred_element_type=F32,
        )
        out_ref[pl.ds(j, layers, stride=SUB), :] = part


def _sweeps(c_ref, f_ref, gx_ref, gy_ref, gz_ref, w_ref, u1_ref, u2_ref, t_ref, lo, hi, ends):
    lo, hi = lo - 2, hi + 2

    def faces(layer, count):
        shape = (count, SUB, LANES)
        sub, lane = _iota(shape, 1), _iota(shape, 2)
        x, y = lane % 32, sub * 4 + lane // 32
        c = _load(c_ref, layer, count)
        after, before = _load(c_ref, layer + 1, count), _load(c_ref, layer - 1, count)
        gx = jnp.where(x < 31, 0.5 * (c + _next_x(c)), 0.0)
        gy = jnp.where(y < 31, 0.5 * (c + _next_y(c)), 0.0)
        gz, gz_before = 0.5 * (c + after), 0.5 * (c + before)
        outer = (x == 0).astype(F32) + (x == 31).astype(F32) + (y == 0).astype(F32) + (y == 31).astype(F32)
        diagonal = gx + _prev_x(gx) + gy + _prev_y(gy) + c * outer
        if ends:
            diagonal = diagonal + jnp.where(after > 0, gz, c) + jnp.where(before > 0, gz_before, c)
            diagonal = jnp.where(c > 0, diagonal, 1.0)
            gz = jnp.where((c > 0) & (after > 0), gz, 0.0)
        else:
            diagonal = diagonal + gz + gz_before
        weight = WEIGHT / diagonal
        _store(gx_ref, layer, gx)
        _store(gy_ref, layer, gy)
        _store(gz_ref, layer, gz)
        _store(w_ref, layer, weight)
        _store(u1_ref, layer, weight * _load(f_ref, layer, count))

    _chunks(lo, hi, 5, faces)
    lo, hi = lo + 1, hi - 1

    def second(layer, count):
        pulled = _pull(u1_ref, gx_ref, gy_ref, gz_ref, layer, count)
        f = _load(f_ref, layer, count)
        _store(u2_ref, layer, _load(w_ref, layer, count) * ((2.0 - WEIGHT) * f + pulled))
        _store(t_ref, layer, (1.0 - WEIGHT) ** 2 * f - WEIGHT * pulled)

    _chunks(lo, hi, 7, second)


def _pull(u_ref, gx_ref, gy_ref, gz_ref, layer, count):
    u = _load(u_ref, layer, count)
    gx, gy = _load(gx_ref, layer, count), _load(gy_ref, layer, count)
    total = gx * _next_x(u) + _prev_x(gx * u)
    total = total + gy * _next_y(u) + _prev_y(gy * u)
    total = total + _load(gz_ref, layer, count) * _load(u_ref, layer + 1, count)
    return total + _load(gz_ref, layer - 1, count) * _load(u_ref, layer - 1, count)


def _residual(u2_ref, t_ref, gx_ref, gy_ref, gz_ref, pair_ref, out_ref, lo, hi, pair_at, out_at):
    def body(layer, count):
        left = _load(t_ref, layer, count) + _pull(u2_ref, gx_ref, gy_ref, gz_ref, layer, count)
        pairs = left.reshape(count // 2, 2, SUB, LANES)
        _store(pair_ref, (layer - lo) // 2 + pair_at, pairs[:, 0] + pairs[:, 1])
        rows = _load(u2_ref, layer, count).reshape(count * SUB, LANES).astype(BF16)
        out_ref[pl.ds(pl.multiple_of((layer - lo + out_at) * SUB, 16), count * SUB), :] = rows

    _chunks(lo, hi, 8, body)


def _pooled(pair_ref, rows):
    lane, to = _iota((LANES, LANES), 0), _iota((LANES, LANES), 1)
    place = (lane // 64) * 16 + (lane % 32) // 2
    total = jnp.zeros((rows, LANES), F32)
    for k in range(4):
        part = pair_ref[pl.ds(k, rows, stride=4), :]
        pick = jnp.where(to == place + 32 * k, 0.125, 0.0).astype(BF16)
        high = part.astype(BF16)
        rest = part - high.astype(F32)
        low = rest.astype(BF16)
        lowest = (rest - low.astype(F32)).astype(BF16)
        for term in (high, low, lowest):
            total = total + jnp.dot(term, pick, preferred_element_type=F32)
    return total


def edges_kernel(layers, f_in, c_in, first_ref, last_ref, f_ref, c_ref):
    def layer_of(row):
        return jnp.where(row < HALO, row, jnp.where(row < 2 * HALO, row + layers - 2 * HALO, -1))

    rows = HALO * SUB
    for at, (cells, ref) in enumerate(((f_in, f_ref), (c_in, c_ref))):
        _transposed(cells, ref, layer_of, 8)
        edges = ref[: 2 * rows, :].astype(BF16)
        first_ref[at * rows : (at + 1) * rows, :] = edges[:rows]
        last_ref[at * rows : (at + 1) * rows, :] = edges[rows:]


def inner_kernel(layers, boxes, owner_ref, f_in, c_in, near_ref, sent_ref, coarse_ref, c_ref, f_ref, *work):
    for cells, ref in ((f_in, f_ref), (c_in, c_ref)):
        _transposed(cells, ref, lambda row: row, layers)
    rows = (EDGE + HALO) * SUB
    for at, ref in enumerate((f_ref, c_ref)):
        near_ref[2 * at * rows : (2 * at + 1) * rows, :] = ref[:rows, :].astype(BF16)
        near_ref[(2 * at + 1) * rows : (2 * at + 2) * rows, :] = ref[layers * SUB - rows :, :].astype(BF16)
    gx, gy, gz, w, u1, u2, t, pair = work
    _sweeps(c_ref, f_ref, gx, gy, gz, w, u1, u2, t, EDGE - 1, layers - EDGE + 1, False)
    blank = EDGE // 2 * SUB
    pair[:blank, :] = jnp.zeros((blank, LANES), F32)
    pair[layers // 2 * SUB - blank :, :] = jnp.zeros((blank, LANES), F32)
    _residual(u2, t, gx, gy, gz, pair, sent_ref, EDGE, layers - EDGE, EDGE // 2, EDGE)
    coarse_ref[...] = _pooled(pair, coarse_ref.shape[0])
    sent_ref[: EDGE * SUB, :] = jnp.zeros((EDGE * SUB, LANES), BF16)
    sent_ref[(layers - EDGE) * SUB : layers * SUB, :] = jnp.zeros((EDGE * SUB, LANES), BF16)
    named = _iota((16, LANES), 0)
    owners = jnp.zeros((16, LANES), F32)
    for k in range(boxes):
        owners = jnp.where(named == k, owner_ref[k].astype(F32), owners)
    sent_ref[layers * SUB :, :] = owners.astype(BF16)


def outer_kernel(layers, before_ref, after_ref, near_ref, inner_ref, sent_in, coarse_ref, sent_ref, c_ref, f_ref, gx, gy, gz, w, u1, u2, t, pair, out_ref, sems):
    del sent_in
    span = EDGE + 2 * HALO
    total = 2 * span
    halo, own = HALO * SUB, (EDGE + HALO) * SUB
    for at, ref in enumerate((f_ref, c_ref)):
        ref[:halo, :] = before_ref[at * halo : (at + 1) * halo, :].astype(F32)
        ref[halo : span * SUB, :] = near_ref[2 * at * own : (2 * at + 1) * own, :].astype(F32)
        ref[span * SUB : total * SUB - halo, :] = near_ref[(2 * at + 1) * own : (2 * at + 2) * own, :].astype(F32)
        ref[total * SUB - halo :, :] = after_ref[at * halo : (at + 1) * halo, :].astype(F32)
    _sweeps(c_ref, f_ref, gx, gy, gz, w, u1, u2, t, HALO, total - HALO, True)
    for at in range(2):
        lo = HALO + at * span
        _residual(u2, t, gx, gy, gz, pair, out_ref, lo, lo + EDGE, at * EDGE // 2, at * EDGE)
    copies = []
    for at, row in enumerate((0, (layers - EDGE) * SUB)):
        copies.append(
            pltpu.make_async_copy(
                out_ref.at[pl.ds(at * EDGE * SUB, EDGE * SUB), :],
                sent_ref.at[pl.ds(row, EDGE * SUB), :],
                sems.at[at],
            )
        )
        copies[-1].start()
    outer = _pooled(pair, SUB)
    inner = inner_ref[...]
    peak = jnp.maximum(jnp.max(jnp.abs(outer)), jnp.max(jnp.abs(inner)))
    power = jnp.floor(jnp.log2(jnp.clip(jnp.full((16, LANES), peak, F32), 1e-30, 1e30)))
    scale = jnp.exp2(-power)[:1, :]
    rows = inner.shape[0]
    low = _iota((SUB, LANES), 0) < EDGE
    coarse_ref[:SUB, :] = jnp.where(low, outer, inner[:SUB]) * scale
    coarse_ref[SUB : rows - SUB, :] = inner[SUB : rows - SUB] * scale
    coarse_ref[rows - SUB : rows, :] = jnp.where(low, inner[rows - SUB :], outer) * scale
    coarse_ref[rows:, :] = power
    for copy in copies:
        copy.wait()


def select_kernel(senders, box_rows, boxes, all_ref, out_ref, named_ref, which_ref, table_ref, box_ref, mixed_ref, done_ref, small_sems, in_sems, out_sems):
    rows = boxes * box_rows
    copy = pltpu.make_async_copy(all_ref.at[:, pl.ds(rows, 16), :], named_ref, small_sems.at[0])
    copy.start()
    copy.wait()
    me = lax.axis_index("grp").astype(F32)
    named = named_ref[...].astype(F32)
    number = _iota(named.shape, 1)
    mine = (named == me) & (number < boxes)
    first = jnp.min(jnp.where(mine, number, boxes), axis=1)
    last = jnp.max(jnp.where(mine, number, -1), axis=1)
    which_ref[0:senders, :] = jnp.where(last >= 0, first, -1)
    which_ref[senders : 2 * senders, :] = jnp.where(last > first, last, -1)
    copy = pltpu.make_async_copy(which_ref, table_ref, small_sems.at[1])
    copy.start()
    copy.wait()

    def fetch(sender, rank):
        box = jnp.maximum(table_ref[rank * senders + sender, 0], 0)
        start = pl.multiple_of(box * box_rows, box_rows)
        return pltpu.make_async_copy(
            all_ref.at[sender, pl.ds(start, box_rows), :], box_ref.at[sender, rank], in_sems.at[sender, rank]
        )

    for sender in range(senders):
        for rank in range(2):
            fetch(sender, rank).start()
    for sender in range(senders):
        for rank in range(2):
            fetch(sender, rank).wait()
            there = (table_ref[rank * senders + sender, 0] >= 0).astype(F32)
            mixed_ref[sender % 2, pl.ds(rank, box_rows, stride=2), :] = jnp.where(there > 0, box_ref[sender, rank].astype(F32), 0.0)
        done_ref[sender] = mixed_ref[sender % 2].astype(BF16)
        pltpu.make_async_copy(done_ref.at[sender], out_ref.at[sender], out_sems.at[sender]).start()
    for sender in range(senders):
        pltpu.make_async_copy(done_ref.at[sender], out_ref.at[sender], out_sems.at[sender]).wait()


def spread_kernel(sizes, block_rows, box_rows, boxes, in_ref, out_ref, mixed_ref):
    step = pl.program_id(0)
    x_count, y_count, core_count = sizes
    row = 0
    for d in range(8):
        device = step * 8 + d
        core, y, x = device % core_count, device // core_count % y_count, device // core_count // y_count
        start = ((y * core_count + core) * x_count + x) * block_rows
        power = in_ref[pl.ds(pl.multiple_of(start + boxes * box_rows, 16), 16), :]
        scale = jnp.exp2(power)[:1, :]
        for k in range(boxes):
            part = in_ref[pl.ds(pl.multiple_of(start + k * box_rows, 16), box_rows), :]
            mixed_ref[row * box_rows : (row + 1) * box_rows, :] = part * scale
            row += 1
    for group in range(row // 8):
        for lane in range(box_rows):
            tile = mixed_ref[pl.ds(group * 8 * box_rows + lane, 8, stride=box_rows), :]
            out_ref[group * 8 : (group + 1) * 8, lane * LANES : (lane + 1) * LANES] = tile


def _params():
    return pltpu.CompilerParams(vmem_limit_bytes=VMEM_LIMIT)


def _whole(count):
    return [pl.BlockSpec(memory_space=pltpu.VMEM)] * count


def _scratch(layers, pair_layers):
    return [pltpu.VMEM((layers * SUB, LANES), F32)] * 9 + [pltpu.VMEM((pair_layers * SUB, LANES), F32)]


def shards(sizes, source, conductivity, new_owner):
    layers, rows_y, rows_x = source.shape
    boxes = new_owner.shape[2]
    depth = layers // boxes
    group_count = lax.axis_size("grp")
    box_rows = depth * SUB
    coarse_rows = depth * SUB * LANES // 8 // LANES
    inner_boxes = boxes - 2
    f_in = jnp.transpose(source, (1, 2, 0)).reshape(rows_y * rows_x, layers)
    c_in = jnp.transpose(conductivity, (1, 2, 0)).reshape(rows_y * rows_x, layers)
    owners = new_owner.reshape(boxes)

    edge = jax.ShapeDtypeStruct((2 * HALO * SUB, LANES), BF16)
    first, last = pl.pallas_call(
        functools.partial(edges_kernel, layers),
        out_shape=[edge, edge],
        in_specs=_whole(2),
        out_specs=_whole(2),
        scratch_shapes=[pltpu.VMEM((8 * SUB, LANES), F32)] * 2,
        compiler_params=_params(),
        cost_estimate=pl.CostEstimate(flops=10**7, bytes_accessed=10**6, transcendentals=0),
        name="edge_layers",
    )(f_in, c_in)
    everyone = ("x", "y", "core", "grp")
    count = lax.axis_size(everyone)
    before = lax.ppermute(last, everyone, [(i, i + 1) for i in range(count - 1)])
    after = lax.ppermute(first, everyone, [(i + 1, i) for i in range(count - 1)])

    sent_shape = jax.ShapeDtypeStruct((boxes * box_rows + 16, LANES), BF16)
    near, sent, coarse_inner = pl.pallas_call(
        functools.partial(inner_kernel, layers, boxes),
        out_shape=[
            jax.ShapeDtypeStruct((4 * (EDGE + HALO) * SUB, LANES), BF16),
            sent_shape,
            jax.ShapeDtypeStruct((boxes * coarse_rows, LANES), F32),
        ],
        in_specs=[pl.BlockSpec(memory_space=pltpu.SMEM)] + _whole(2),
        out_specs=_whole(3),
        scratch_shapes=_scratch(layers, layers // 2),
        compiler_params=_params(),
        cost_estimate=pl.CostEstimate(flops=10**8, bytes_accessed=10**7, transcendentals=0),
        name="inner_layers",
    )(owners, f_in, c_in)

    total = 2 * (EDGE + 2 * HALO)
    coarse, sent = pl.pallas_call(
        functools.partial(outer_kernel, layers),
        out_shape=[jax.ShapeDtypeStruct((boxes * coarse_rows + 16, LANES), F32), sent_shape],
        in_specs=_whole(4) + [pl.BlockSpec(memory_space=pl.ANY)],
        out_specs=_whole(1) + [pl.BlockSpec(memory_space=pl.ANY)],
        scratch_shapes=_scratch(total, EDGE)
        + [pltpu.VMEM((2 * EDGE * SUB, LANES), BF16), pltpu.SemaphoreType.DMA((2,))],
        input_output_aliases={4: 1},
        compiler_params=_params(),
        name="outer_layers",
    )(before, after, near, coarse_inner, sent)

    got = lax.all_gather(sent, "grp", axis=0, tiled=True)
    gathered = coarse.astype(F16)
    for axes in ("x", ("y", "core")):
        gathered = lax.all_gather(gathered, axes, axis=0, tiled=True)

    senders = group_count
    correction = pl.pallas_call(
        functools.partial(select_kernel, senders, box_rows, boxes),
        out_shape=jax.ShapeDtypeStruct((senders, 2 * box_rows, LANES), BF16),
        in_specs=[pl.BlockSpec(memory_space=pltpu.HBM)],
        out_specs=pl.BlockSpec(memory_space=pl.ANY),
        scratch_shapes=[
            pltpu.VMEM((senders, 16, LANES), BF16),
            pltpu.VMEM((2 * senders, LANES), jnp.int32),
            pltpu.SMEM((2 * senders, LANES), jnp.int32),
            pltpu.VMEM((senders, 2, box_rows, LANES), BF16),
            pltpu.VMEM((2, 2 * box_rows, LANES), F32),
            pltpu.VMEM((senders, 2 * box_rows, LANES), BF16),
            pltpu.SemaphoreType.DMA((2,)),
            pltpu.SemaphoreType.DMA((senders, 2)),
            pltpu.SemaphoreType.DMA((senders,)),
        ],
        compiler_params=_params(),
        name="select_boxes",
    )(got.reshape(senders, boxes * box_rows + 16, LANES))
    correction = correction.reshape(senders, box_rows, 2, LANES).transpose(0, 2, 1, 3)

    devices = sizes[0] * sizes[1] * sizes[2]
    coarse_all = pl.pallas_call(
        functools.partial(spread_kernel, sizes, coarse.shape[0], coarse_rows, boxes),
        out_shape=jax.ShapeDtypeStruct((devices * boxes, coarse_rows * LANES), F32),
        grid=(devices // 8,),
        in_specs=_whole(1),
        out_specs=pl.BlockSpec((8 * boxes, coarse_rows * LANES), lambda i: (i, 0)),
        scratch_shapes=[pltpu.VMEM((8 * boxes * coarse_rows, LANES), F32)],
        compiler_params=_params(),
        name="spread_coarse",
    )(gathered.astype(F32))
    return (
        correction.reshape(1, 1, senders, 2, box_rows * LANES),
        coarse_all[None],
    )


def solution(mesh):
    sizes = (4, 8, 2) if mesh.shape["box"] == 64 else (1, 8, 2)
    fine = Mesh(mesh.devices.reshape(sizes + (mesh.shape["grp"],)), ("x", "y", "core", "grp"))
    box = ("x", "y", "core")
    return jax.shard_map(
        functools.partial(shards, sizes),
        mesh=fine,
        in_specs=(
            P(box + ("grp",), None, None),
            P(box + ("grp",), None, None),
            P(box, "grp", None, None),
        ),
        out_specs=(P(box, "grp", None, None, None), P("grp", None, None)),
        check_vma=False,
    )
```

time: 247 us -> 117 us (0.47)
  waiting for transfers between devices: 110 us -> 19.9 us
  local copies, waits for them, and re-layouts: 43.2 us -> 4.85 us
  other arithmetic: 29.5 us -> 0.41 us
  Pallas kernels: 0 us -> 24.3 us
  blocking collectives: 23.8 us -> 35.8 us
  matrix products: 5.7 us -> 0 us
    all_gather x2 -> x1, waiting for transfers between devices: 98.8 us -> 19.9 us  [shards(): got = lax.all_gather(sent, 'grp', axis=0, tiled=True)]
    all_gather x0 -> x2, blocking collectives: none -> 35.8 us  [shards(): gathered = lax.all_gather(gathered, axes, axis=0, tiled=True)]
    pallas_call x0 -> x5, Pallas kernels: none -> 24.3 us  [the longest x1 12 us: shards(): pl.pallas_call(functools.partial(inner_kernel, layers, boxes), out_shape=...]
    another operation x1 -> x0, local copies, waits for them, and re-layouts: 23.9 us -> none  [restrict(): leftover.reshape(leading + (layers // 2, 2, rows_y // 2, 2, rows_x // 2, 2))]
    unnamed x1 -> x0, blocking collectives: 23.8 us -> none
    reduce_sum x2 -> x0, other arithmetic: 15.6 us -> none  [the longest x1 15.5 us: restrict(): return jnp.mean(blocks, axis=(-5, -3, -1)).reshape(leading + (-1,))]
    ppermute x2, waiting for transfers between devices: 11.5 us -> 0.01 us  [the longest x1 0.01 us: shards(): lax.ppermute(last, everyone, [(i, i + 1) for i in range(count - 1)])]
    select_n x5 -> x0, other arithmetic: 6.51 us -> none  [the longest x1 2.25 us: smooth(): leftover = jnp.where(inside, source - operate(sweep_two), 0.0)]
  transfers between devices with their start and end apart: 4 -> 3, of which waited for: 4 -> 1; matrix products, arithmetic and copies ran while one was open for 22% -> 0% of each run, Pallas kernels for 0% -> 15%
where the time goes in v1:
time: 117 us; the launch traced here: 116 us
  blocking collectives  35.8 us (31%)
  Pallas kernels  24.3 us (21%)
  waiting for transfers between devices  19.9 us (17%)
  starting transfers between devices  16.8 us (14%)
  between operations  14.1 us (12%)
  local copies, waits for them, and re-layouts  4.85 us (4%)
    all_gather x2, blocking collectives, shards(): gathered = lax.all_gather(gathered, axes, axis=0, tiled=True)  35.8 us
    all_gather x1, waiting for transfers between devices, shards(): got = lax.all_gather(sent, 'grp', axis=0, tiled=True)  19.9 us
    ppermute x1, starting transfers between devices, shards(): lax.ppermute(first, everyone, [(i + 1, i) for i in range(count - 1)])  12.5 us
    pallas_call x1, Pallas kernels, shards(): pl.pallas_call(functools.partial(inner_kernel, layers, boxes), out_shape=...  12 us
    pallas_call x1, Pallas kernels, shards(): pl.pallas_call(functools.partial(spread_kernel, sizes, coarse.shape[0], c...  5.66 us
    unnamed x8, local copies, waits for them, and re-layouts  4.85 us
    pallas_call x1, Pallas kernels, shards(): pl.pallas_call(functools.partial(select_kernel, senders, box_rows, boxes)...  4.52 us
    ppermute x1, starting transfers between devices, shards(): lax.ppermute(last, everyone, [(i, i + 1) for i in range(count - 1)])  4.29 us
  transfers between devices with their start and end apart: 3, of which 1 were waited for; matrix products, arithmetic and copies ran while one was open for 0% of the time, Pallas kernels for 15%

profile of v1, /device:TPU:56, one launch (start us, length us, event | category | flops | bytes accessed | tf_op | source)
XLA Modules:
  0.0 116.0 jit_solution(6523780108563960444)
XLA Ops:
  7.2 0.0 all-gather.3.cloned.1.call-start
  7.2 0.0 copy-start.1
  7.2 1.0 copy-done.1
  8.3 0.0 copy-start.2
  8.3 1.0 copy-done.2
  9.3 0.4 edge_layers.1
  9.7 4.3 %collective-permute-start = (bf16[48,128]{1,0:T(8,128)(2,1)S(1)}, bf16[48,128]{1,0:T(8,128)(2,1)S(1)}, u32[]{:S(2)}, u32[]{:S(2)}) collective-permute-start(bf16[48,128]{1,0:T(8,128)(2,1)S(1)} %get-tuple-element.9), channel_id=1, source_target_pairs={{0,1},{1,2},{2,3},{3,4},{4,5},{5,6},{6,7},{7,8},{8,9},{9,10},{10,1... | collective-permute-start | bytes 36872 | tf_op jit(solution)/shard_map/ppermute | solution.py:326
  14.0 12.5 %collective-permute-start.1 = (bf16[48,128]{1,0:T(8,128)(2,1)S(1)}, bf16[48,128]{1,0:T(8,128)(2,1)S(1)}, u32[]{:S(2)}, u32[]{:S(2)}) collective-permute-start(bf16[48,128]{1,0:T(8,128)(2,1)S(1)} %get-tuple-element.10), channel_id=1, source_target_pairs={{1,0},{2,1},{3,2},{4,3},{5,4},{6,5},{7,6},{8,7},{9,8},{10,9},{11,1... | collective-permute-start | bytes 36872 | tf_op jit(solution)/shard_map/ppermute | solution.py:327
  26.4 0.0 copy-start.3
  26.4 0.6 copy-done.3
  27.1 12.0 %inner_layers.1 = (bf16[224,128]{1,0:T(8,128)(2,1)S(1)}, bf16[1296,128]{1,0:T(8,128)(2,1)}, f32[160,128]{1,0:T(8,128)S(1)}) custom-call(s32[5]{0:T(128)S(1)} %bitcast.19, bf16[1024,160]{1,0:T(8,128)(2,1)S(1)} %bitcast.16, bf16[1024,160]{1,0:T(8,128)(2,1)S(1)} %bitcast.18), custom_call_target="tpu_custom_call" | custom-call | flops 100000000 | bytes 10000000 | tf_op jit(solution)/shard_map/inner_layers/pallas_call | solution.py:330
  39.1 0.0 collective-permute-done.before_ref
  39.1 0.0 collective-permute-done.1.after_ref
  39.1 1.7 %outer_layers.1 = (f32[176,128]{1,0:T(8,128)S(1)}, bf16[1296,128]{1,0:T(8,128)(2,1)}) custom-call(bf16[48,128]{1,0:T(8,128)(2,1)S(1)} %collective-permute-done.before_ref, bf16[48,128]{1,0:T(8,128)(2,1)S(1)} %collective-permute-done.1.after_ref, bf16[224,128]{1,0:T(8,128)(2,1)S(1)} %get-tuple-element.11.near_ref, ...), custom_call_target="tpu_custom_call", output_to_operand_aliasing={{1}: (4, {})} | custom-call | tf_op jit(solution)/shard_map/outer_layers/pallas_call | solution.py:346
  40.8 0.0 all-gather.3.cloned.1.call-update
  40.8 12.4 %all_gather.10 = f16[704,128]{1,0:T(8,128)(2,1)S(1)} all-gather(f16[176,128]{1,0:T(8,128)(2,1)S(1)} %convert_element_type.6), channel_id=1, replica_groups=mesh['x'=4,'y'=8,'core'=2,'grp'=12] {'x'}, dimensions={0}, use_global_device_ids=true | all-gather | bytes 225280 | tf_op jit(solution)/shard_map/all_gather | solution.py:361
  53.3 23.3 %all-gather.4 = f16[11264,128]{1,0:T(8,128)(2,1)S(1)} all-gather(f16[704,128]{1,0:T(8,128)(2,1)S(1)} %all_gather.10), channel_id=1, replica_groups=mesh['x'=4,'y'=8,'core'=2,'grp'=12] {'y','core'}, dimensions={0}, use_global_device_ids=true | all-gather | bytes 3063808 | tf_op jit(solution)/shard_map/all_gather | solution.py:361
  76.6 0.4 convert_element_type.7.in_ref
  77.0 5.7 %spread_coarse.1 = f32[320,4096]{1,0:T(8,128)} custom-call(f32[11264,128]{1,0:T(8,128)S(1)} %convert_element_type.7.in_ref), custom_call_target="tpu_custom_call" | custom-call | tf_op jit(solution)/shard_map/spread_coarse/pallas_call | solution.py:386
  82.7 19.9 %all-gather.3.cloned.1.call-done = bf16[15552,128]{1,0:T(8,128)(2,1)} async-done(((bf16[1296,128]{1,0:T(8,128)(2,1)}), bf16[15552,128]{1,0:T(8,128)(2,1)}) %all-gather.3.cloned.1.call-update) | async-done | bytes 3981328 | tf_op jit(solution)/shard_map/all_gather | solution.py:358
  102.5 0.0 copy-start
  102.5 2.1 %copy-done = bf16[15552,128]{1,0:T(8,128)(2,1)S(1)} copy-done((bf16[15552,128]{1,0:T(8,128)(2,1)S(1)}, bf16[15552,128]{1,0:T(8,128)(2,1)}, u32[]{:S(2)}) %copy-start) | copy-done | bytes 3981336
  104.7 4.5 %select_boxes.1 = bf16[12,512,128]{2,1,0:T(8,128)(2,1)} custom-call(bf16[12,1296,128]{2,1,0:T(8,128)(2,1)S(1)} %bitcast.14), custom_call_target="tpu_custom_call" | custom-call | tf_op jit(solution)/shard_map/select_boxes/pallas_call | solution.py:364
  (1 shorter events, 0.0 us)
Async XLA Ops:
  7.2 95.4 %all-gather.3.cloned.1.call-start = ((), (), s32[]{:S(2)}) async-start(), calls=%async_computation | async-start | bytes 4313088 | tf_op jit(solution)/shard_map/all_gather | solution.py:358
  7.2 1.0 copy-start.1
  8.3 1.0 copy-start.2
  9.7 29.4 %collective-permute-start = (bf16[48,128]{1,0:T(8,128)(2,1)S(1)}, bf16[48,128]{1,0:T(8,128)(2,1)S(1)}, u32[]{:S(2)}, u32[]{:S(2)}) collective-permute-start(bf16[48,128]{1,0:T(8,128)(2,1)S(1)} %get-tuple-element.9), channel_id=1, source_target_pairs={{0,1},{1,2},{2,3},{3,4},{4,5},{5,6},{6,7},{7,8},{8,9},{9,10},{10,1... | collective-permute-start | bytes 36872 | tf_op jit(solution)/shard_map/ppermute | solution.py:326
  14.0 25.1 %collective-permute-start.1 = (bf16[48,128]{1,0:T(8,128)(2,1)S(1)}, bf16[48,128]{1,0:T(8,128)(2,1)S(1)}, u32[]{:S(2)}, u32[]{:S(2)}) collective-permute-start(bf16[48,128]{1,0:T(8,128)(2,1)S(1)} %get-tuple-element.10), channel_id=1, source_target_pairs={{1,0},{2,1},{3,2},{4,3},{5,4},{6,5},{7,6},{8,7},{9,8},{10,9},{11,1... | collective-permute-start | bytes 36872 | tf_op jit(solution)/shard_map/ppermute | solution.py:327
  26.4 0.7 copy-start.3
  102.5 2.1 %copy-start = (bf16[15552,128]{1,0:T(8,128)(2,1)S(1)}, bf16[15552,128]{1,0:T(8,128)(2,1)}, u32[]{:S(2)}) copy-start(bf16[15552,128]{1,0:T(8,128)(2,1)} %all-gather.3.cloned.1.call-done) | copy-start | bytes 11943940
Sparse Core Ops, SparseCore 0:
  40.9 61.5 all-gather.2

commit v2 on v1

v2 whole, which is shorter than its diff:
```python
import functools

import jax
import jax.numpy as jnp
from jax import lax
from jax.experimental import pallas as pl
from jax.experimental.pallas import tpu as pltpu
from jax.sharding import Mesh, PartitionSpec as P

WEIGHT = 0.8
F32, BF16, F16 = jnp.float32, jnp.bfloat16, jnp.float16
HALO = 3
STEP = 40
EDGE = 2
SIDE = 4
SUB, LANES = 8, 128
VMEM_LIMIT = 40 * 1024 * 1024


def _iota(shape, dim):
    return lax.broadcasted_iota(jnp.int32, shape, dim)


def _chunks(lo, hi, step, body):
    whole = (hi - lo) // step
    if whole:

        @pl.loop(0, whole)
        def _(i):
            body(lo + i * step, step)

    if lo + whole * step < hi:
        body(lo + whole * step, hi - lo - whole * step)


def _load(ref, layer, count, shift=0):
    if isinstance(layer, int):
        rows = ref[layer * SUB + shift : (layer + count) * SUB + shift, :]
    elif shift:
        rows = ref[pl.ds(layer * SUB + shift, count * SUB), :]
    else:
        rows = ref[pl.ds(pl.multiple_of(layer * SUB, SUB), count * SUB), :]
    return rows.reshape(count, SUB, LANES)


def _store(ref, layer, value):
    count = value.shape[0]
    rows = value.reshape(count * SUB, LANES)
    if isinstance(layer, int):
        ref[layer * SUB : (layer + count) * SUB, :] = rows
    else:
        ref[pl.ds(pl.multiple_of(layer * SUB, SUB), count * SUB), :] = rows


def _beside(ref, layer, count):
    here = _load(ref, layer, count)
    lane = _iota((1, SUB, LANES), 2)
    below = jnp.where(lane < 32, _load(ref, layer, count, 1), here)
    above = jnp.where(lane >= 96, _load(ref, layer, count, -1), here)
    return (
        pltpu.roll(here, LANES - 1, 2),
        pltpu.roll(here, 1, 2),
        pltpu.roll(below, LANES - 32, 2),
        pltpu.roll(above, 32, 2),
    )


def _transposed(cells_ref, out_ref, layer_of, layers, at=0):
    total = cells_ref.shape[1]
    pick = (_iota((layers, total), 1) == layer_of(_iota((layers, total), 0))).astype(BF16)
    for j in range(SUB):
        part = lax.dot_general(
            pick,
            cells_ref[j * LANES : (j + 1) * LANES, :],
            (((1,), (1,)), ((), ())),
            preferred_element_type=F32,
        )
        out_ref[pl.ds(at * SUB + j, layers, stride=SUB), :] = part


def _sweeps(c_ref, f_ref, g_refs, gz_ref, w_ref, u1_ref, u2_ref, t_ref, lo, hi, ends):
    lo, hi = lo - 2, hi + 2
    sub, lane = _iota((1, SUB, LANES), 1), _iota((1, SUB, LANES), 2)
    x, y = lane & 31, sub * 4 + (lane >> 5)
    sides = (x == 31, x == 0, y == 31, y == 0)
    halves = [jnp.where(side, 0.0, 0.5) for side in sides]
    outer = sum(side.astype(F32) for side in sides)

    def faces(layer, count):
        c = _load(c_ref, layer, count)
        after, before = _load(c_ref, layer + 1, count), _load(c_ref, layer - 1, count)
        gz, gz_before = 0.5 * (c + after), 0.5 * (c + before)
        diagonal = c * outer
        if ends:
            diagonal = diagonal + jnp.where(after > 0, gz, c) + jnp.where(before > 0, gz_before, c)
            gz = jnp.where((c > 0) & (after > 0), gz, 0.0)
        else:
            diagonal = diagonal + (gz + gz_before)
        _store(gz_ref, layer, gz)
        for half, g_ref, other in zip(halves, g_refs, _beside(c_ref, layer, count)):
            g = half * (c + other)
            diagonal = diagonal + g
            _store(g_ref, layer, g)
        if ends:
            diagonal = jnp.where(c > 0, diagonal, 1.0)
        inverse = pl.reciprocal(diagonal, approx=True)
        inverse = inverse * (2.0 - diagonal * inverse)
        inverse = inverse * (2.0 - diagonal * inverse)
        weight = WEIGHT * inverse
        _store(w_ref, layer, weight)
        _store(u1_ref, layer, weight * _load(f_ref, layer, count))

    _chunks(lo, hi, STEP, faces)
    lo, hi = lo + 1, hi - 1

    def second(layer, count):
        pulled = _pull(u1_ref, g_refs, gz_ref, layer, count)
        f = _load(f_ref, layer, count)
        _store(u2_ref, layer, _load(w_ref, layer, count) * ((2.0 - WEIGHT) * f + pulled))
        if t_ref is not None:
            _store(t_ref, layer, (1.0 - WEIGHT) ** 2 * f - WEIGHT * pulled)

    _chunks(lo, hi, STEP, second)


def _pull(u_ref, g_refs, gz_ref, layer, count):
    total = _load(gz_ref, layer, count) * _load(u_ref, layer + 1, count)
    total = total + _load(gz_ref, layer - 1, count) * _load(u_ref, layer - 1, count)
    for g_ref, other in zip(g_refs, _beside(u_ref, layer, count)):
        total = total + _load(g_ref, layer, count) * other
    return total


def _residual(u2_ref, t_ref, g_refs, gz_ref, pair_ref, lo, hi, pair_at):
    def body(layer, count):
        left = _load(t_ref, layer, count) + _pull(u2_ref, g_refs, gz_ref, layer, count)
        pairs = left.reshape(count // 2, 2, SUB, LANES)
        _store(pair_ref, (layer - lo) // 2 + pair_at, pairs[:, 0] + pairs[:, 1])

    _chunks(lo, hi, STEP, body)


def _pooled(pair_ref, rows):
    lane, to = _iota((LANES, LANES), 0), _iota((LANES, LANES), 1)
    place = (lane // 64) * 16 + (lane % 32) // 2
    total = jnp.zeros((rows, LANES), F32)
    for k in range(4):
        part = pair_ref[pl.ds(k, rows, stride=4), :]
        pick = jnp.where(to == place + 32 * k, 0.125, 0.0).astype(BF16)
        high = part.astype(BF16)
        rest = part - high.astype(F32)
        low = rest.astype(BF16)
        lowest = (rest - low.astype(F32)).astype(BF16)
        for term in (high, low, lowest):
            total = total + jnp.dot(term, pick, preferred_element_type=F32)
    return total


def edges_kernel(layers, f_in, c_in, first_ref, last_ref, f_held, c_held, f_ref, c_ref, sems):
    def layer_of(row):
        return jnp.where(row < SIDE, row, row + layers - 2 * SIDE)

    copies = [
        pltpu.make_async_copy(cells, held, sems.at[at])
        for at, (cells, held) in enumerate(((f_in, f_held), (c_in, c_held)))
    ]
    for copy in copies:
        copy.start()
    rows = SIDE * SUB
    for at, (copy, held, ref) in enumerate(zip(copies, (f_held, c_held), (f_ref, c_ref))):
        copy.wait()
        _transposed(held, ref, layer_of, 2 * SIDE)
        first_ref[at * rows : (at + 1) * rows, :] = ref[:rows, :].astype(BF16)
        last_ref[at * rows : (at + 1) * rows, :] = ref[rows:, :].astype(BF16)


def _halo(side_ref, at, last):
    rows = SIDE * SUB
    cells = side_ref[at * rows : (at + 1) * rows, :].astype(F32)
    return cells[rows - HALO * SUB :] if last else cells[: HALO * SUB]


def inner_kernel(layers, f_in, c_in, near_ref, u2_ref, c_ref, f_ref, *work):
    for cells, ref in ((f_in, f_ref), (c_in, c_ref)):
        _transposed(cells, ref, lambda row: row, layers)
    rows = (EDGE + HALO) * SUB
    for at, ref in enumerate((f_ref, c_ref)):
        near_ref[2 * at * rows : (2 * at + 1) * rows, :] = ref[:rows, :]
        near_ref[(2 * at + 1) * rows : (2 * at + 2) * rows, :] = ref[layers * SUB - rows :, :]
    *g, gz, w, u1 = work
    _sweeps(c_ref, f_ref, g, gz, w, u1, u2_ref, None, EDGE + 1, layers - EDGE - 1, False)
    u2_ref[: EDGE * SUB, :] = jnp.zeros((EDGE * SUB, LANES), F32)
    u2_ref[(layers - EDGE) * SUB : layers * SUB, :] = jnp.zeros((EDGE * SUB, LANES), F32)


def outer_kernel(layers, box_rows, boxes, owner_ref, before_ref, after_ref, near_ref, u2_in, slots_ref, c_ref, f_ref, *work):
    *g, gz, w, u1, u2, settled_ref, mixed_ref = work
    span = EDGE + 2 * HALO
    total = 2 * span
    halo, own = HALO * SUB, (EDGE + HALO) * SUB
    for at, ref in enumerate((f_ref, c_ref)):
        ref[:halo, :] = _halo(before_ref, at, True)
        ref[halo : span * SUB, :] = near_ref[2 * at * own : (2 * at + 1) * own, :]
        ref[span * SUB : total * SUB - halo, :] = near_ref[(2 * at + 1) * own : (2 * at + 2) * own, :]
        ref[total * SUB - halo :, :] = _halo(after_ref, at, False)
    _sweeps(c_ref, f_ref, g, gz, w, u1, u2, None, HALO, total - HALO, True)

    rows = layers * SUB
    edge = EDGE * SUB
    settled_ref[edge : rows - edge, :] = u2_in[edge : rows - edge, :]
    settled_ref[:edge, :] = u2[halo : halo + edge, :]
    settled_ref[rows - edge :, :] = u2[span * SUB + halo : span * SUB + halo + edge, :]
    slots_ref[...] = jnp.zeros(slots_ref.shape, BF16)
    for k in range(boxes):
        owner = owner_ref[k]
        seen = jnp.int32(0)
        for j in range(k):
            seen = jnp.where(owner_ref[j] == owner, 1, seen)
        second = jnp.int32(-1)
        for j in range(k + 1, boxes):
            second = jnp.where(owner_ref[j] == owner, j, second)

        @pl.when(seen == 0)
        def _():
            mixed_ref[pl.ds(0, box_rows, stride=2), :] = settled_ref[k * box_rows : (k + 1) * box_rows, :]

            @pl.when(second < 0)
            def _():
                mixed_ref[pl.ds(1, box_rows, stride=2), :] = jnp.zeros((box_rows, LANES), F32)

            @pl.when(second >= 0)
            def _():
                start = pl.multiple_of(jnp.maximum(second, 0) * box_rows, box_rows)
                mixed_ref[pl.ds(1, box_rows, stride=2), :] = settled_ref[pl.ds(start, box_rows), :]

            slots_ref[owner] = mixed_ref[...].astype(BF16)


def coarse_kernel(layers, before_ref, after_ref, f_in, c_in, coarse_ref, c_ref, f_ref, *work):
    *g, gz, w, u1, t, u2, pair = work
    halo, rows = HALO * SUB, layers * SUB
    for at, (cells, ref) in enumerate(((f_in, f_ref), (c_in, c_ref))):
        _transposed(cells, ref, lambda row: row, layers, HALO)
        ref[:halo, :] = _halo(before_ref, at, True)
        ref[halo + rows :, :] = _halo(after_ref, at, False)
    _sweeps(c_ref, f_ref, g, gz, w, u1, u2, t, HALO, HALO + layers, True)
    _residual(u2, t, g, gz, pair, HALO, HALO + layers, 0)
    rows = coarse_ref.shape[0] - 16
    means = _pooled(pair, rows)
    peak = jnp.full((16, LANES), jnp.max(jnp.abs(means)), F32)
    power = jnp.floor(jnp.log2(jnp.clip(peak, 1e-30, 1e30)))
    coarse_ref[:rows, :] = means * jnp.exp2(-power)[:1, :]
    coarse_ref[rows:, :] = power


def spread_kernel(sizes, block_rows, box_rows, boxes, in_ref, out_ref, mixed_ref):
    step = pl.program_id(0)
    x_count, y_count, core_count = sizes
    row = 0
    for d in range(8):
        device = step * 8 + d
        core, y, x = device % core_count, device // core_count % y_count, device // core_count // y_count
        start = ((y * core_count + core) * x_count + x) * block_rows
        power = in_ref[pl.ds(pl.multiple_of(start + boxes * box_rows, 16), 16), :]
        scale = jnp.exp2(power)[:1, :]
        for k in range(boxes):
            part = in_ref[pl.ds(pl.multiple_of(start + k * box_rows, 16), box_rows), :]
            mixed_ref[row * box_rows : (row + 1) * box_rows, :] = part * scale
            row += 1
    for group in range(row // 8):
        for lane in range(box_rows):
            tile = mixed_ref[pl.ds(group * 8 * box_rows + lane, 8, stride=box_rows), :]
            out_ref[group * 8 : (group + 1) * 8, lane * LANES : (lane + 1) * LANES] = tile


def _params(limit=VMEM_LIMIT):
    return pltpu.CompilerParams(vmem_limit_bytes=limit)


def _whole(count):
    return [pl.BlockSpec(memory_space=pltpu.VMEM)] * count


def _scratch(layers, count):
    return [pltpu.VMEM((layers * SUB, LANES), F32)] * count


def shards(sizes, source, conductivity, new_owner):
    layers, rows_y, rows_x = source.shape
    boxes = new_owner.shape[2]
    depth = layers // boxes
    group_count = lax.axis_size("grp")
    box_rows = depth * SUB
    coarse_rows = depth * SUB * LANES // 8 // LANES
    inner_boxes = boxes - 2
    f_in = jnp.transpose(source, (1, 2, 0)).reshape(rows_y * rows_x, layers)
    c_in = jnp.transpose(conductivity, (1, 2, 0)).reshape(rows_y * rows_x, layers)
    owners = new_owner.reshape(boxes)

    edge = jax.ShapeDtypeStruct((2 * SIDE * SUB, LANES), BF16)
    held = jax.ShapeDtypeStruct(f_in.shape, BF16)
    first, last, f_held, c_held = pl.pallas_call(
        functools.partial(edges_kernel, layers),
        out_shape=[edge, edge, held, held],
        in_specs=[pl.BlockSpec(memory_space=pltpu.HBM)] * 2,
        out_specs=_whole(4),
        scratch_shapes=_scratch(2 * SIDE, 2) + [pltpu.SemaphoreType.DMA((2,))],
        compiler_params=_params(),
        cost_estimate=pl.CostEstimate(flops=10**7, bytes_accessed=10**6, transcendentals=0),
        name="edge_layers",
    )(*(pltpu.with_memory_space_constraint(cells, pltpu.HBM) for cells in (f_in, c_in)))
    everyone = ("x", "y", "core", "grp")
    count = lax.axis_size(everyone)
    before = lax.ppermute(last, everyone, [(i, i + 1) for i in range(count - 1)])
    after = lax.ppermute(first, everyone, [(i + 1, i) for i in range(count - 1)])

    near, u2 = pl.pallas_call(
        functools.partial(inner_kernel, layers),
        out_shape=[
            jax.ShapeDtypeStruct((4 * (EDGE + HALO) * SUB, LANES), F32),
            jax.ShapeDtypeStruct((layers * SUB, LANES), F32),
        ],
        in_specs=_whole(2),
        out_specs=_whole(2),
        scratch_shapes=_scratch(layers, 9),
        compiler_params=_params(),
        cost_estimate=pl.CostEstimate(flops=10**8, bytes_accessed=10**7, transcendentals=0),
        name="inner_layers",
    )(f_held, c_held)

    total = 2 * (EDGE + 2 * HALO)
    slots = pl.pallas_call(
        functools.partial(outer_kernel, layers, box_rows, boxes),
        out_shape=jax.ShapeDtypeStruct((group_count, 2 * box_rows, LANES), BF16),
        in_specs=[pl.BlockSpec(memory_space=pltpu.SMEM)] + _whole(4),
        out_specs=pl.BlockSpec(memory_space=pltpu.VMEM),
        scratch_shapes=_scratch(total, 10) + _scratch(layers, 1) + _scratch(2 * depth, 1),
        compiler_params=_params(),
        name="outer_layers",
    )(owners, before, after, near, u2)

    coarse = pl.pallas_call(
        functools.partial(coarse_kernel, layers),
        out_shape=jax.ShapeDtypeStruct((boxes * coarse_rows + 16, LANES), F32),
        in_specs=_whole(4),
        out_specs=pl.BlockSpec(memory_space=pltpu.VMEM),
        scratch_shapes=_scratch(layers + 2 * HALO, 11) + _scratch(layers // 2, 1),
        compiler_params=_params(),
        cost_estimate=pl.CostEstimate(flops=10**8, bytes_accessed=10**7, transcendentals=0),
        name="coarse_rows",
    )(before, after, f_held, c_held)

    correction = lax.all_to_all(slots, "grp", split_axis=0, concat_axis=0, tiled=True)
    correction = correction.reshape(group_count, box_rows, 2, LANES).transpose(0, 2, 1, 3)
    gathered = coarse.astype(F16)
    for axes in ("x", ("y", "core")):
        gathered = lax.all_gather(gathered, axes, axis=0, tiled=True)

    devices = sizes[0] * sizes[1] * sizes[2]
    coarse_all = pl.pallas_call(
        functools.partial(spread_kernel, sizes, coarse.shape[0], coarse_rows, boxes),
        out_shape=jax.ShapeDtypeStruct((devices * boxes, coarse_rows * LANES), F32),
        grid=(devices // 8,),
        in_specs=_whole(1),
        out_specs=pl.BlockSpec((8 * boxes, coarse_rows * LANES), lambda i: (i, 0)),
        scratch_shapes=[pltpu.VMEM((8 * boxes * coarse_rows, LANES), F32)],
        compiler_params=_params(),
        name="spread_coarse",
    )(gathered.astype(F32))
    return (
        correction.reshape(1, 1, group_count, 2, box_rows * LANES),
        coarse_all[None],
    )


def solution(mesh):
    sizes = (4, 8, 2) if mesh.shape["box"] == 64 else (1, 8, 2)
    fine = Mesh(mesh.devices.reshape(sizes + (mesh.shape["grp"],)), ("x", "y", "core", "grp"))
    box = ("x", "y", "core")
    return jax.shard_map(
        functools.partial(shards, sizes),
        mesh=fine,
        in_specs=(
            P(box + ("grp",), None, None),
            P(box + ("grp",), None, None),
            P(box, "grp", None, None),
        ),
        out_specs=(P(box, "grp", None, None, None), P("grp", None, None)),
        check_vma=False,
    )
```

time: 117 us -> 89.7 us (0.77)
  between operations: 14.1 us -> 0.72 us
  waiting for transfers between devices: 19.9 us -> 11.1 us
  Pallas kernels: 24.3 us -> 16.6 us
  starting transfers between devices: 16.8 us -> 22.8 us
  local copies, waits for them, and re-layouts: 4.85 us -> 1.79 us
    all_gather x1 -> x0, waiting for transfers between devices: 19.9 us -> none  [shards(): got = lax.all_gather(sent, 'grp', axis=0, tiled=True)]
    all_to_all x0 -> x1, waiting for transfers between devices: none -> 11.1 us  [shards(): lax.all_to_all(slots, 'grp', split_axis=0, concat_axis=0, tiled=True)]
    pallas_call x3, Pallas kernels: 18.2 us -> 9.39 us  [the longest x1 4.63 us: shards(): pl.pallas_call(functools.partial(coarse_kernel, layers), out_shape=jax.Sh...]
    all_to_all x0 -> x1, starting transfers between devices: none -> 6.1 us  [shards(): lax.all_to_all(slots, 'grp', split_axis=0, concat_axis=0, tiled=True)]
    unnamed x8 -> x3, local copies, waits for them, and re-layouts: 4.85 us -> 1.79 us
    pallas_call x1, Pallas kernels: 0.38 us -> 1.57 us  [shards(): pl.pallas_call(functools.partial(edges_kernel, layers), out_shape=[edge,...]
  transfers between devices with their start and end apart: 3 -> 3, of which waited for: 1 -> 1; matrix products, arithmetic and copies ran while one was open for 0% -> 0% of each run, Pallas kernels for 15% -> 14%
where the time goes in v2:
time: 89.7 us; the launch traced here: 89.5 us
  blocking collectives  35.9 us (40%)
  starting transfers between devices  22.8 us (25%)
  Pallas kernels  16.6 us (19%)
  waiting for transfers between devices  11.1 us (12%)
  local copies, waits for them, and re-layouts  1.79 us (2%)
    all_gather x2, blocking collectives, shards(): gathered = lax.all_gather(gathered, axes, axis=0, tiled=True)  35.9 us
    ppermute x1, starting transfers between devices, shards(): lax.ppermute(first, everyone, [(i + 1, i) for i in range(count - 1)])  12.5 us
    all_to_all x1, waiting for transfers between devices, shards(): lax.all_to_all(slots, 'grp', split_axis=0, concat_axis=0, tiled=True)  11.1 us
    all_to_all x1, starting transfers between devices, shards(): lax.all_to_all(slots, 'grp', split_axis=0, concat_axis=0, tiled=True)  6.1 us
    pallas_call x1, Pallas kernels, shards(): pl.pallas_call(functools.partial(spread_kernel, sizes, coarse.shape[0], c...  5.66 us
    pallas_call x1, Pallas kernels, shards(): pl.pallas_call(functools.partial(coarse_kernel, layers), out_shape=jax.Sh...  4.63 us
    ppermute x1, starting transfers between devices, shards(): lax.ppermute(last, everyone, [(i, i + 1) for i in range(count - 1)])  4.28 us
    pallas_call x1, Pallas kernels, shards(): pl.pallas_call(functools.partial(inner_kernel, layers), out_shape=[jax.Sh...  2.52 us
  transfers between devices with their start and end apart: 3, of which 1 were waited for; matrix products, arithmetic and copies ran while one was open for 0% of the time, Pallas kernels for 14%

profile of v2, /device:TPU:56, one launch (start us, length us, event | category | flops | bytes accessed | tf_op | source)
XLA Modules:
  0.0 89.5 jit_solution(3509769052345083029)
XLA Ops:
  0.6 1.6 %edge_layers.1 = (bf16[64,128]{1,0:T(8,128)(2,1)S(1)}, bf16[64,128]{1,0:T(8,128)(2,1)S(1)}, bf16[1024,160]{1,0:T(8,128)(2,1)S(1)}, bf16[1024,160]{1,0:T(8,128)(2,1)S(1)}) custom-call(bf16[1024,160]{1,0:T(8,128)(2,1)} %bitcast.16, bf16[1024,160]{1,0:T(8,128)(2,1)} %bitcast.17), custom_call_target="tpu_custom_call" | custom-call | flops 10000000 | bytes 1000000 | tf_op jit(solution)/shard_map/edge_layers/pallas_call | solution.py:302
  2.2 4.3 %collective-permute-start = (bf16[64,128]{1,0:T(8,128)(2,1)S(1)}, bf16[64,128]{1,0:T(8,128)(2,1)S(1)}, u32[]{:S(2)}, u32[]{:S(2)}) collective-permute-start(bf16[64,128]{1,0:T(8,128)(2,1)S(1)} %get-tuple-element.8), channel_id=1, source_target_pairs={{0,1},{1,2},{2,3},{3,4},{4,5},{5,6},{6,7},{7,8},{8,9},{9,10},{10,1... | collective-permute-start | bytes 49160 | tf_op jit(solution)/shard_map/ppermute | solution.py:314
  6.5 12.5 %collective-permute-start.1 = (bf16[64,128]{1,0:T(8,128)(2,1)S(1)}, bf16[64,128]{1,0:T(8,128)(2,1)S(1)}, u32[]{:S(2)}, u32[]{:S(2)}) collective-permute-start(bf16[64,128]{1,0:T(8,128)(2,1)S(1)} %get-tuple-element.9), channel_id=1, source_target_pairs={{1,0},{2,1},{3,2},{4,3},{5,4},{6,5},{7,6},{8,7},{9,8},{10,9},{11,1... | collective-permute-start | bytes 49160 | tf_op jit(solution)/shard_map/ppermute | solution.py:315
  19.0 2.5 %inner_layers.1 = (f32[160,128]{1,0:T(8,128)S(1)}, f32[1280,128]{1,0:T(8,128)S(1)}) custom-call(bf16[1024,160]{1,0:T(8,128)(2,1)S(1)} %get-tuple-element.10.f_in, bf16[1024,160]{1,0:T(8,128)(2,1)S(1)} %get-tuple-element.11.c_in), custom_call_target="tpu_custom_call" | custom-call | flops 100000000 | bytes 10000000 | tf_op jit(solution)/shard_map/inner_layers/pallas_call | solution.py:317
  21.5 0.0 collective-permute-done.before_ref
  21.5 0.0 collective-permute-done.1.after_ref
  21.5 0.0 copy-start
  21.5 0.6 copy-done
  22.2 2.2 %outer_layers.1 = bf16[12,512,128]{2,1,0:T(8,128)(2,1)} custom-call(s32[5]{0:T(128)S(1)} %bitcast.13, bf16[64,128]{1,0:T(8,128)(2,1)S(1)} %collective-permute-done.before_ref, bf16[64,128]{1,0:T(8,128)(2,1)S(1)} %collective-permute-done.1.after_ref, f32[160,128]{1,0:T(8,128)S(1)} %get-tuple-element.12.near_ref, f32[1280,128]{1,0:T(8,128)S(1)} %get-tuple-element.13.u2_in), custom_call_target="tpu_custom_call" | custom-call | tf_op jit(solution)/shard_map/outer_layers/pallas_call | solution.py:332
  24.4 6.1 %all-to-all-start = ((bf16[12,512,128]{2,1,0:T(8,128)(2,1)}), bf16[12,512,128]{2,1,0:T(8,128)(2,1)S(1)}, u32[]{:S(2)}, u32[]{:S(2)}) async-start(bf16[12,512,128]{2,1,0:T(8,128)(2,1)} %outer_layers.1), calls=%async_computation | async-start | bytes 3145728 | tf_op jit(solution)/shard_map/all_to_all | solution.py:353
  30.5 4.6 %coarse_rows.1 = f32[176,128]{1,0:T(8,128)S(1)} custom-call(bf16[64,128]{1,0:T(8,128)(2,1)S(1)} %collective-permute-done.before_ref, bf16[64,128]{1,0:T(8,128)(2,1)S(1)} %collective-permute-done.1.after_ref, bf16[1024,160]{1,0:T(8,128)(2,1)S(1)} %get-tuple-element.10.f_in, bf16[1024,160]{1,0:T(8,128)(2,1)S(1)} %get-tuple-element.11.c_in), custom_call_target="tpu_custom_call" | custom-call | flops 100000000 | bytes 10000000 | tf_op jit(solution)/shard_map/coarse_rows/pallas_call | solution.py:342
  35.2 12.7 %all_gather.6 = f16[704,128]{1,0:T(8,128)(2,1)S(1)} all-gather(f16[176,128]{1,0:T(8,128)(2,1)S(1)} %convert_element_type.6), channel_id=1, replica_groups=mesh['x'=4,'y'=8,'core'=2,'grp'=12] {'x'}, dimensions={0}, use_global_device_ids=true | all-gather | bytes 225280 | tf_op jit(solution)/shard_map/all_gather | solution.py:357
  47.8 23.3 %all-gather.1 = f16[11264,128]{1,0:T(8,128)(2,1)S(1)} all-gather(f16[704,128]{1,0:T(8,128)(2,1)S(1)} %all_gather.6), channel_id=1, replica_groups=mesh['x'=4,'y'=8,'core'=2,'grp'=12] {'y','core'}, dimensions={0}, use_global_device_ids=true | all-gather | bytes 3063808 | tf_op jit(solution)/shard_map/all_gather | solution.py:357
  71.1 0.4 convert_element_type.7.in_ref
  71.5 5.7 %spread_coarse.1 = f32[320,4096]{1,0:T(8,128)} custom-call(f32[11264,128]{1,0:T(8,128)S(1)} %convert_element_type.7.in_ref), custom_call_target="tpu_custom_call" | custom-call | tf_op jit(solution)/shard_map/spread_coarse/pallas_call | solution.py:360
  77.2 11.1 %all-to-all-done = bf16[12,512,128]{2,1,0:T(8,128)(2,1)S(1)} async-done(((bf16[12,512,128]{2,1,0:T(8,128)(2,1)}), bf16[12,512,128]{2,1,0:T(8,128)(2,1)S(1)}, u32[]{:S(2)}, u32[]{:S(2)}) %all-to-all-start) | async-done | bytes 1572896 | tf_op jit(solution)/shard_map/all_to_all | solution.py:353
  88.3 1.1 %copy.7 = bf16[1,1,12,2,32768]{4,3,2,1,0:T(2,128)(2,1)} copy(bf16[1,1,12,2,32768]{4,3,2,1,0:T(2,128)(2,1)S(1)} %bitcast.14) | data formatting | bytes 3145728
  (1 shorter events, 0.0 us)
Async XLA Ops:
  2.2 19.3 %collective-permute-start = (bf16[64,128]{1,0:T(8,128)(2,1)S(1)}, bf16[64,128]{1,0:T(8,128)(2,1)S(1)}, u32[]{:S(2)}, u32[]{:S(2)}) collective-permute-start(bf16[64,128]{1,0:T(8,128)(2,1)S(1)} %get-tuple-element.8), channel_id=1, source_target_pairs={{0,1},{1,2},{2,3},{3,4},{4,5},{5,6},{6,7},{7,8},{8,9},{9,10},{10,1... | collective-permute-start | bytes 49160 | tf_op jit(solution)/shard_map/ppermute | solution.py:314
  6.5 15.0 %collective-permute-start.1 = (bf16[64,128]{1,0:T(8,128)(2,1)S(1)}, bf16[64,128]{1,0:T(8,128)(2,1)S(1)}, u32[]{:S(2)}, u32[]{:S(2)}) collective-permute-start(bf16[64,128]{1,0:T(8,128)(2,1)S(1)} %get-tuple-element.9), channel_id=1, source_target_pairs={{1,0},{2,1},{3,2},{4,3},{5,4},{6,5},{7,6},{8,7},{9,8},{10,9},{11,1... | collective-permute-start | bytes 49160 | tf_op jit(solution)/shard_map/ppermute | solution.py:315
  21.5 0.7 copy-start
  24.4 63.9 %all-to-all-start = ((bf16[12,512,128]{2,1,0:T(8,128)(2,1)}), bf16[12,512,128]{2,1,0:T(8,128)(2,1)S(1)}, u32[]{:S(2)}, u32[]{:S(2)}) async-start(bf16[12,512,128]{2,1,0:T(8,128)(2,1)} %outer_layers.1), calls=%async_computation | async-start | bytes 3145728 | tf_op jit(solution)/shard_map/all_to_all | solution.py:353

commit v3 on v2

--- a/solution.py
+++ b/solution.py
@@ -193,8 +193,10 @@
     u2_ref[(layers - EDGE) * SUB : layers * SUB, :] = jnp.zeros((EDGE * SUB, LANES), F32)
 
 
-def outer_kernel(layers, box_rows, boxes, owner_ref, before_ref, after_ref, near_ref, u2_in, slots_ref, c_ref, f_ref, *work):
-    *g, gz, w, u1, u2, settled_ref, mixed_ref = work
+def outer_kernel(layers, box_rows, boxes, owner_in, before_ref, after_ref, near_ref, u2_in, slots_ref, c_ref, f_ref, *work):
+    *g, gz, w, u1, u2, settled_ref, mixed_ref, staged_ref, owner_ref, owner_sem, sems = work
+    load = pltpu.make_async_copy(owner_in, owner_ref, owner_sem.at[0])
+    load.start()
     span = EDGE + 2 * HALO
     total = 2 * span
     halo, own = HALO * SUB, (EDGE + HALO) * SUB
@@ -204,36 +206,38 @@
         ref[span * SUB : total * SUB - halo, :] = near_ref[(2 * at + 1) * own : (2 * at + 2) * own, :]
         ref[total * SUB - halo :, :] = _halo(after_ref, at, False)
     _sweeps(c_ref, f_ref, g, gz, w, u1, u2, None, HALO, total - HALO, True)
-
     rows = layers * SUB
     edge = EDGE * SUB
     settled_ref[edge : rows - edge, :] = u2_in[edge : rows - edge, :]
     settled_ref[:edge, :] = u2[halo : halo + edge, :]
     settled_ref[rows - edge :, :] = u2[span * SUB + halo : span * SUB + halo + edge, :]
-    slots_ref[...] = jnp.zeros(slots_ref.shape, BF16)
-    for k in range(boxes):
-        owner = owner_ref[k]
-        seen = jnp.int32(0)
-        for j in range(k):
-            seen = jnp.where(owner_ref[j] == owner, 1, seen)
-        second = jnp.int32(-1)
-        for j in range(k + 1, boxes):
-            second = jnp.where(owner_ref[j] == owner, j, second)
-
-        @pl.when(seen == 0)
+    load.wait()
+
+    owners = [owner_ref[0, k] for k in range(boxes)]
+    sends = []
+    for owner in range(slots_ref.shape[0]):
+        first, second = jnp.int32(-1), jnp.int32(-1)
+        for k in range(boxes):
+            named = owners[k] == owner
+            second = jnp.where(named & (first >= 0), k, second)
+            first = jnp.where(named & (first < 0), k, first)
+
+        @pl.when(first < 0)
         def _():
-            mixed_ref[pl.ds(0, box_rows, stride=2), :] = settled_ref[k * box_rows : (k + 1) * box_rows, :]
-
-            @pl.when(second < 0)
-            def _():
-                mixed_ref[pl.ds(1, box_rows, stride=2), :] = jnp.zeros((box_rows, LANES), F32)
-
-            @pl.when(second >= 0)
-            def _():
-                start = pl.multiple_of(jnp.maximum(second, 0) * box_rows, box_rows)
-                mixed_ref[pl.ds(1, box_rows, stride=2), :] = settled_ref[pl.ds(start, box_rows), :]
-
-            slots_ref[owner] = mixed_ref[...].astype(BF16)
+            staged_ref[owner] = jnp.zeros((2 * box_rows, LANES), BF16)
+
+        @pl.when(first >= 0)
+        def _():
+            for rank, box in enumerate((first, second)):
+                start = pl.multiple_of(jnp.maximum(box, 0) * box_rows, box_rows)
+                cells = settled_ref[pl.ds(start, box_rows), :]
+                mixed_ref[pl.ds(rank, box_rows, stride=2), :] = cells if rank == 0 else jnp.where(box >= 0, cells, 0.0)
+            staged_ref[owner] = mixed_ref[...].astype(BF16)
+
+        sends.append(pltpu.make_async_copy(staged_ref.at[owner], slots_ref.at[owner], sems.at[owner]))
+        sends[-1].start()
+    for send in sends:
+        send.wait()
 
 
 def coarse_kernel(layers, before_ref, after_ref, f_in, c_in, coarse_ref, c_ref, f_ref, *work):
@@ -253,10 +257,10 @@
     coarse_ref[rows:, :] = power
 
 
-def spread_kernel(sizes, block_rows, box_rows, boxes, in_ref, out_ref, mixed_ref):
+def spread_kernel(sizes, block_rows, box_rows, boxes, in_ref, out_ref):
     step = pl.program_id(0)
     x_count, y_count, core_count = sizes
-    row = 0
+    parts = []
     for d in range(8):
         device = step * 8 + d
         core, y, x = device % core_count, device // core_count % y_count, device // core_count // y_count
@@ -264,13 +268,11 @@
         power = in_ref[pl.ds(pl.multiple_of(start + boxes * box_rows, 16), 16), :]
         scale = jnp.exp2(power)[:1, :]
         for k in range(boxes):
-            part = in_ref[pl.ds(pl.multiple_of(start + k * box_rows, 16), box_rows), :]
-            mixed_ref[row * box_rows : (row + 1) * box_rows, :] = part * scale
-            row += 1
-    for group in range(row // 8):
+            parts.append(in_ref[pl.ds(pl.multiple_of(start + k * box_rows, 16), box_rows), :] * scale)
+    for at in range(0, len(parts), 8):
+        tiles = jnp.swapaxes(jnp.stack(parts[at : at + 8]), 0, 1)
         for lane in range(box_rows):
-            tile = mixed_ref[pl.ds(group * 8 * box_rows + lane, 8, stride=box_rows), :]
-            out_ref[group * 8 : (group + 1) * 8, lane * LANES : (lane + 1) * LANES] = tile
+            out_ref[at : at + 8, lane * LANES : (lane + 1) * LANES] = tiles[lane]
 
 
 def _params(limit=VMEM_LIMIT):
@@ -295,7 +297,7 @@
     inner_boxes = boxes - 2
     f_in = jnp.transpose(source, (1, 2, 0)).reshape(rows_y * rows_x, layers)
     c_in = jnp.transpose(conductivity, (1, 2, 0)).reshape(rows_y * rows_x, layers)
-    owners = new_owner.reshape(boxes)
+    owners = new_owner.reshape(1, boxes)
 
     edge = jax.ShapeDtypeStruct((2 * SIDE * SUB, LANES), BF16)
     held = jax.ShapeDtypeStruct(f_in.shape, BF16)
@@ -329,15 +331,24 @@
     )(f_held, c_held)
 
     total = 2 * (EDGE + 2 * HALO)
+    slots_shape = (group_count, 2 * box_rows, LANES)
     slots = pl.pallas_call(
         functools.partial(outer_kernel, layers, box_rows, boxes),
-        out_shape=jax.ShapeDtypeStruct((group_count, 2 * box_rows, LANES), BF16),
-        in_specs=[pl.BlockSpec(memory_space=pltpu.SMEM)] + _whole(4),
-        out_specs=pl.BlockSpec(memory_space=pltpu.VMEM),
-        scratch_shapes=_scratch(total, 10) + _scratch(layers, 1) + _scratch(2 * depth, 1),
+        out_shape=jax.ShapeDtypeStruct(slots_shape, BF16),
+        in_specs=[pl.BlockSpec(memory_space=pltpu.HBM)] + _whole(4),
+        out_specs=pl.BlockSpec(memory_space=pltpu.HBM),
+        scratch_shapes=_scratch(total, 10)
+        + _scratch(layers, 1)
+        + _scratch(2 * depth, 1)
+        + [
+            pltpu.VMEM(slots_shape, BF16),
+            pltpu.SMEM((1, boxes), jnp.int32),
+            pltpu.SemaphoreType.DMA((1,)),
+            pltpu.SemaphoreType.DMA((group_count,)),
+        ],
         compiler_params=_params(),
         name="outer_layers",
-    )(owners, before, after, near, u2)
+    )(pltpu.with_memory_space_constraint(owners, pltpu.HBM), before, after, near, u2)
 
     coarse = pl.pallas_call(
         functools.partial(coarse_kernel, layers),
@@ -363,7 +374,6 @@
         grid=(devices // 8,),
         in_specs=_whole(1),
         out_specs=pl.BlockSpec((8 * boxes, coarse_rows * LANES), lambda i: (i, 0)),
-        scratch_shapes=[pltpu.VMEM((8 * boxes * coarse_rows, LANES), F32)],
         compiler_params=_params(),
         name="spread_coarse",
     )(gathered.astype(F32))

time: 89.7 us -> 88.8 us (0.990)
  Pallas kernels: 16.6 us -> 14.9 us
  waiting for transfers between devices: 11.1 us -> 12.8 us
    all_to_all x1, waiting for transfers between devices: 11.1 us -> 12.8 us  [shards(): lax.all_to_all(slots, 'grp', split_axis=0, concat_axis=0, tiled=True)]
    pallas_call x1, Pallas kernels: 5.66 us -> 4.19 us  [shards(): pl.pallas_call(functools.partial(spread_kernel, sizes, coarse.shape[0], c...]
  transfers between devices with their start and end apart: 3 -> 3, of which waited for: 1 -> 1; matrix products, arithmetic and copies ran while one was open for 0% -> 0% of each run, Pallas kernels for 14% -> 13%
where the time goes in v3:
time: 88.8 us; the launch traced here: 88.6 us
  blocking collectives  35.8 us (40%)
  starting transfers between devices  22.9 us (26%)
  Pallas kernels  14.9 us (17%)
  waiting for transfers between devices  12.8 us (14%)
  local copies, waits for them, and re-layouts  1.14 us (1%)
    all_gather x2, blocking collectives, shards(): gathered = lax.all_gather(gathered, axes, axis=0, tiled=True)  35.8 us
    all_to_all x1, waiting for transfers between devices, shards(): lax.all_to_all(slots, 'grp', split_axis=0, concat_axis=0, tiled=True)  12.8 us
    ppermute x1, starting transfers between devices, shards(): lax.ppermute(first, everyone, [(i + 1, i) for i in range(count - 1)])  12.5 us
    all_to_all x1, starting transfers between devices, shards(): lax.all_to_all(slots, 'grp', split_axis=0, concat_axis=0, tiled=True)  6.12 us
    pallas_call x1, Pallas kernels, shards(): pl.pallas_call(functools.partial(coarse_kernel, layers), out_shape=jax.Sh...  4.63 us
    ppermute x1, starting transfers between devices, shards(): lax.ppermute(last, everyone, [(i, i + 1) for i in range(count - 1)])  4.28 us
    pallas_call x1, Pallas kernels, shards(): pl.pallas_call(functools.partial(spread_kernel, sizes, coarse.shape[0], c...  4.19 us
    pallas_call x1, Pallas kernels, shards(): pl.pallas_call(functools.partial(inner_kernel, layers), out_shape=[jax.Sh...  2.52 us
  transfers between devices with their start and end apart: 3, of which 1 were waited for; matrix products, arithmetic and copies ran while one was open for 0% of the time, Pallas kernels for 13%

profile of v3, /device:TPU:56, one launch (start us, length us, event | category | flops | bytes accessed | tf_op | source)
XLA Modules:
  0.0 88.6 jit_solution(6714052004466849964)
XLA Ops:
  0.6 1.6 %edge_layers.1 = (bf16[64,128]{1,0:T(8,128)(2,1)S(1)}, bf16[64,128]{1,0:T(8,128)(2,1)S(1)}, bf16[1024,160]{1,0:T(8,128)(2,1)S(1)}, bf16[1024,160]{1,0:T(8,128)(2,1)S(1)}) custom-call(bf16[1024,160]{1,0:T(8,128)(2,1)} %bitcast.15, bf16[1024,160]{1,0:T(8,128)(2,1)} %bitcast.16), custom_call_target="tpu_custom_call" | custom-call | flops 10000000 | bytes 1000000 | tf_op jit(solution)/shard_map/edge_layers/pallas_call | solution.py:304
  2.2 4.3 %collective-permute-start = (bf16[64,128]{1,0:T(8,128)(2,1)S(1)}, bf16[64,128]{1,0:T(8,128)(2,1)S(1)}, u32[]{:S(2)}, u32[]{:S(2)}) collective-permute-start(bf16[64,128]{1,0:T(8,128)(2,1)S(1)} %get-tuple-element.8), channel_id=1, source_target_pairs={{0,1},{1,2},{2,3},{3,4},{4,5},{5,6},{6,7},{7,8},{8,9},{9,10},{10,1... | collective-permute-start | bytes 49160 | tf_op jit(solution)/shard_map/ppermute | solution.py:316
  6.5 12.5 %collective-permute-start.1 = (bf16[64,128]{1,0:T(8,128)(2,1)S(1)}, bf16[64,128]{1,0:T(8,128)(2,1)S(1)}, u32[]{:S(2)}, u32[]{:S(2)}) collective-permute-start(bf16[64,128]{1,0:T(8,128)(2,1)S(1)} %get-tuple-element.9), channel_id=1, source_target_pairs={{1,0},{2,1},{3,2},{4,3},{5,4},{6,5},{7,6},{8,7},{9,8},{10,9},{11,1... | collective-permute-start | bytes 49160 | tf_op jit(solution)/shard_map/ppermute | solution.py:317
  19.0 2.5 %inner_layers.1 = (f32[160,128]{1,0:T(8,128)S(1)}, f32[1280,128]{1,0:T(8,128)S(1)}) custom-call(bf16[1024,160]{1,0:T(8,128)(2,1)S(1)} %get-tuple-element.10.f_in, bf16[1024,160]{1,0:T(8,128)(2,1)S(1)} %get-tuple-element.11.c_in), custom_call_target="tpu_custom_call" | custom-call | flops 100000000 | bytes 10000000 | tf_op jit(solution)/shard_map/inner_layers/pallas_call | solution.py:319
  21.5 0.0 collective-permute-done.before_ref
  21.5 0.0 collective-permute-done.1.after_ref
  21.5 2.0 %outer_layers.1 = bf16[12,512,128]{2,1,0:T(8,128)(2,1)} custom-call(s32[1,5]{1,0:T(1,128)} %bitcast.17, bf16[64,128]{1,0:T(8,128)(2,1)S(1)} %collective-permute-done.before_ref, bf16[64,128]{1,0:T(8,128)(2,1)S(1)} %collective-permute-done.1.after_ref, f32[160,128]{1,0:T(8,128)S(1)} %get-tuple-element.12.near_ref, f32[1280,128]{1,0:T(8,128)S(1)} %get-tuple-element.13.u2_in), custom_call_target="tpu_custom_call" | custom-call | tf_op jit(solution)/shard_map/outer_layers/pallas_call | solution.py:335
  23.5 6.1 %all-to-all-start = ((bf16[12,512,128]{2,1,0:T(8,128)(2,1)}), bf16[12,512,128]{2,1,0:T(8,128)(2,1)S(1)}, u32[]{:S(2)}, u32[]{:S(2)}) async-start(bf16[12,512,128]{2,1,0:T(8,128)(2,1)} %outer_layers.1), calls=%async_computation | async-start | bytes 3145728 | tf_op jit(solution)/shard_map/all_to_all | solution.py:364
  29.6 4.6 %coarse_rows.1 = f32[176,128]{1,0:T(8,128)S(1)} custom-call(bf16[64,128]{1,0:T(8,128)(2,1)S(1)} %collective-permute-done.before_ref, bf16[64,128]{1,0:T(8,128)(2,1)S(1)} %collective-permute-done.1.after_ref, bf16[1024,160]{1,0:T(8,128)(2,1)S(1)} %get-tuple-element.10.f_in, bf16[1024,160]{1,0:T(8,128)(2,1)S(1)} %get-tuple-element.11.c_in), custom_call_target="tpu_custom_call" | custom-call | flops 100000000 | bytes 10000000 | tf_op jit(solution)/shard_map/coarse_rows/pallas_call | solution.py:353
  34.2 12.7 %all_gather.6 = f16[704,128]{1,0:T(8,128)(2,1)S(1)} all-gather(f16[176,128]{1,0:T(8,128)(2,1)S(1)} %convert_element_type.6), channel_id=1, replica_groups=mesh['x'=4,'y'=8,'core'=2,'grp'=12] {'x'}, dimensions={0}, use_global_device_ids=true | all-gather | bytes 225280 | tf_op jit(solution)/shard_map/all_gather | solution.py:368
  46.9 23.1 %all-gather.1 = f16[11264,128]{1,0:T(8,128)(2,1)S(1)} all-gather(f16[704,128]{1,0:T(8,128)(2,1)S(1)} %all_gather.6), channel_id=1, replica_groups=mesh['x'=4,'y'=8,'core'=2,'grp'=12] {'y','core'}, dimensions={0}, use_global_device_ids=true | all-gather | bytes 3063808 | tf_op jit(solution)/shard_map/all_gather | solution.py:368
  70.0 0.4 convert_element_type.7.in_ref
  70.4 4.2 %spread_coarse.1 = f32[320,4096]{1,0:T(8,128)} custom-call(f32[11264,128]{1,0:T(8,128)S(1)} %convert_element_type.7.in_ref), custom_call_target="tpu_custom_call" | custom-call | tf_op jit(solution)/shard_map/spread_coarse/pallas_call | solution.py:371
  74.6 12.8 %all-to-all-done = bf16[12,512,128]{2,1,0:T(8,128)(2,1)S(1)} async-done(((bf16[12,512,128]{2,1,0:T(8,128)(2,1)}), bf16[12,512,128]{2,1,0:T(8,128)(2,1)S(1)}, u32[]{:S(2)}, u32[]{:S(2)}) %all-to-all-start) | async-done | bytes 1572896 | tf_op jit(solution)/shard_map/all_to_all | solution.py:364
  87.5 1.1 %copy.7 = bf16[1,1,12,2,32768]{4,3,2,1,0:T(2,128)(2,1)} copy(bf16[1,1,12,2,32768]{4,3,2,1,0:T(2,128)(2,1)S(1)} %bitcast.13) | data formatting | bytes 3145728
  (1 shorter events, 0.0 us)
Async XLA Ops:
  2.2 19.3 %collective-permute-start = (bf16[64,128]{1,0:T(8,128)(2,1)S(1)}, bf16[64,128]{1,0:T(8,128)(2,1)S(1)}, u32[]{:S(2)}, u32[]{:S(2)}) collective-permute-start(bf16[64,128]{1,0:T(8,128)(2,1)S(1)} %get-tuple-element.8), channel_id=1, source_target_pairs={{0,1},{1,2},{2,3},{3,4},{4,5},{5,6},{6,7},{7,8},{8,9},{9,10},{10,1... | collective-permute-start | bytes 49160 | tf_op jit(solution)/shard_map/ppermute | solution.py:316
  6.5 15.0 %collective-permute-start.1 = (bf16[64,128]{1,0:T(8,128)(2,1)S(1)}, bf16[64,128]{1,0:T(8,128)(2,1)S(1)}, u32[]{:S(2)}, u32[]{:S(2)}) collective-permute-start(bf16[64,128]{1,0:T(8,128)(2,1)S(1)} %get-tuple-element.9), channel_id=1, source_target_pairs={{1,0},{2,1},{3,2},{4,3},{5,4},{6,5},{7,6},{8,7},{9,8},{10,9},{11,1... | collective-permute-start | bytes 49160 | tf_op jit(solution)/shard_map/ppermute | solution.py:317
  23.5 64.0 %all-to-all-start = ((bf16[12,512,128]{2,1,0:T(8,128)(2,1)}), bf16[12,512,128]{2,1,0:T(8,128)(2,1)S(1)}, u32[]{:S(2)}, u32[]{:S(2)}) async-start(bf16[12,512,128]{2,1,0:T(8,128)(2,1)} %outer_layers.1), calls=%async_computation | async-start | bytes 3145728 | tf_op jit(solution)/shard_map/all_to_all | solution.py:364

commit v4 on v3

--- a/solution.py
+++ b/solution.py
@@ -180,20 +180,27 @@
     return cells[rows - HALO * SUB :] if last else cells[: HALO * SUB]
 
 
-def inner_kernel(layers, f_in, c_in, near_ref, u2_ref, c_ref, f_ref, *work):
+def inner_kernel(layers, f_in, c_in, near_ref, u2_ref, slots_ref, c_ref, f_ref, *work):
+    *g, gz, w, u1, blank_ref, sems = work
+    blank_ref[...] = jnp.zeros(blank_ref.shape, BF16)
+    blanks = [pltpu.make_async_copy(blank_ref, slots_ref.at[i], sems.at[i]) for i in range(slots_ref.shape[0])]
+    for copy in blanks:
+        copy.start()
     for cells, ref in ((f_in, f_ref), (c_in, c_ref)):
         _transposed(cells, ref, lambda row: row, layers)
     rows = (EDGE + HALO) * SUB
     for at, ref in enumerate((f_ref, c_ref)):
         near_ref[2 * at * rows : (2 * at + 1) * rows, :] = ref[:rows, :]
         near_ref[(2 * at + 1) * rows : (2 * at + 2) * rows, :] = ref[layers * SUB - rows :, :]
-    *g, gz, w, u1 = work
     _sweeps(c_ref, f_ref, g, gz, w, u1, u2_ref, None, EDGE + 1, layers - EDGE - 1, False)
     u2_ref[: EDGE * SUB, :] = jnp.zeros((EDGE * SUB, LANES), F32)
     u2_ref[(layers - EDGE) * SUB : layers * SUB, :] = jnp.zeros((EDGE * SUB, LANES), F32)
-
-
-def outer_kernel(layers, box_rows, boxes, owner_in, before_ref, after_ref, near_ref, u2_in, slots_ref, c_ref, f_ref, *work):
+    for copy in blanks:
+        copy.wait()
+
+
+def outer_kernel(layers, box_rows, boxes, owner_in, before_ref, after_ref, near_ref, u2_in, slots_in, slots_ref, c_ref, f_ref, *work):
+    del slots_in
     *g, gz, w, u1, u2, settled_ref, mixed_ref, staged_ref, owner_ref, owner_sem, sems = work
     load = pltpu.make_async_copy(owner_in, owner_ref, owner_sem.at[0])
     load.start()
@@ -215,26 +222,23 @@
 
     owners = [owner_ref[0, k] for k in range(boxes)]
     sends = []
-    for owner in range(slots_ref.shape[0]):
-        first, second = jnp.int32(-1), jnp.int32(-1)
-        for k in range(boxes):
-            named = owners[k] == owner
-            second = jnp.where(named & (first >= 0), k, second)
-            first = jnp.where(named & (first < 0), k, first)
-
-        @pl.when(first < 0)
+    for k in range(boxes):
+        first, second = jnp.int32(k), jnp.int32(-1)
+        for j in range(boxes):
+            if j < k:
+                first = jnp.where((owners[j] == owners[k]) & (first == k), j, first)
+            if j > k:
+                second = jnp.where(owners[j] == owners[k], j, second)
+
+        @pl.when(first == k)
         def _():
-            staged_ref[owner] = jnp.zeros((2 * box_rows, LANES), BF16)
-
-        @pl.when(first >= 0)
-        def _():
-            for rank, box in enumerate((first, second)):
-                start = pl.multiple_of(jnp.maximum(box, 0) * box_rows, box_rows)
-                cells = settled_ref[pl.ds(start, box_rows), :]
-                mixed_ref[pl.ds(rank, box_rows, stride=2), :] = cells if rank == 0 else jnp.where(box >= 0, cells, 0.0)
-            staged_ref[owner] = mixed_ref[...].astype(BF16)
-
-        sends.append(pltpu.make_async_copy(staged_ref.at[owner], slots_ref.at[owner], sems.at[owner]))
+            mixed_ref[pl.ds(0, box_rows, stride=2), :] = settled_ref[k * box_rows : (k + 1) * box_rows, :]
+            start = pl.multiple_of(jnp.maximum(second, 0) * box_rows, box_rows)
+            cells = settled_ref[pl.ds(start, box_rows), :]
+            mixed_ref[pl.ds(1, box_rows, stride=2), :] = jnp.where(second >= 0, cells, 0.0)
+            staged_ref[k] = mixed_ref[...].astype(BF16)
+
+        sends.append(pltpu.make_async_copy(staged_ref.at[first], slots_ref.at[owners[k]], sems.at[k]))
         sends[-1].start()
     for send in sends:
         send.wait()
@@ -316,39 +320,50 @@
     before = lax.ppermute(last, everyone, [(i, i + 1) for i in range(count - 1)])
     after = lax.ppermute(first, everyone, [(i + 1, i) for i in range(count - 1)])
 
-    near, u2 = pl.pallas_call(
+    slots_shape = (group_count, 2 * box_rows, LANES)
+    hbm = pl.BlockSpec(memory_space=pltpu.HBM)
+    near, u2, slots = pl.pallas_call(
         functools.partial(inner_kernel, layers),
         out_shape=[
             jax.ShapeDtypeStruct((4 * (EDGE + HALO) * SUB, LANES), F32),
             jax.ShapeDtypeStruct((layers * SUB, LANES), F32),
+            pltpu.HBM(slots_shape, BF16),
         ],
         in_specs=_whole(2),
-        out_specs=_whole(2),
-        scratch_shapes=_scratch(layers, 9),
+        out_specs=_whole(2) + [hbm],
+        scratch_shapes=_scratch(layers, 9)
+        + [pltpu.VMEM(slots_shape[1:], BF16), pltpu.SemaphoreType.DMA((group_count,))],
         compiler_params=_params(),
         cost_estimate=pl.CostEstimate(flops=10**8, bytes_accessed=10**7, transcendentals=0),
         name="inner_layers",
     )(f_held, c_held)
 
     total = 2 * (EDGE + 2 * HALO)
-    slots_shape = (group_count, 2 * box_rows, LANES)
     slots = pl.pallas_call(
         functools.partial(outer_kernel, layers, box_rows, boxes),
         out_shape=jax.ShapeDtypeStruct(slots_shape, BF16),
-        in_specs=[pl.BlockSpec(memory_space=pltpu.HBM)] + _whole(4),
-        out_specs=pl.BlockSpec(memory_space=pltpu.HBM),
+        in_specs=[hbm] + _whole(4) + [hbm],
+        out_specs=hbm,
         scratch_shapes=_scratch(total, 10)
         + _scratch(layers, 1)
         + _scratch(2 * depth, 1)
         + [
-            pltpu.VMEM(slots_shape, BF16),
+            pltpu.VMEM((boxes,) + slots_shape[1:], BF16),
             pltpu.SMEM((1, boxes), jnp.int32),
             pltpu.SemaphoreType.DMA((1,)),
-            pltpu.SemaphoreType.DMA((group_count,)),
+            pltpu.SemaphoreType.DMA((boxes,)),
         ],
+        input_output_aliases={5: 0},
         compiler_params=_params(),
         name="outer_layers",
-    )(pltpu.with_memory_space_constraint(owners, pltpu.HBM), before, after, near, u2)
+    )(
+        pltpu.with_memory_space_constraint(owners, pltpu.HBM),
+        before,
+        after,
+        near,
+        u2,
+        pltpu.with_memory_space_constraint(slots, pltpu.HBM),
+    )
 
     coarse = pl.pallas_call(
         functools.partial(coarse_kernel, layers),

time: 88.8 us -> 88.4 us (level)
  no operation moved by 1% of the time
where the time goes in v4:
time: 88.4 us; the launch traced here: 88.2 us
  blocking collectives  35.9 us (41%)
  starting transfers between devices  22.7 us (26%)
  Pallas kernels  14.6 us (17%)
  waiting for transfers between devices  12.6 us (14%)
  local copies, waits for them, and re-layouts  1.14 us (1%)
    all_gather x2, blocking collectives, shards(): gathered = lax.all_gather(gathered, axes, axis=0, tiled=True)  35.9 us
    all_to_all x1, waiting for transfers between devices, shards(): lax.all_to_all(slots, 'grp', split_axis=0, concat_axis=0, tiled=True)  12.6 us
    ppermute x1, starting transfers between devices, shards(): lax.ppermute(first, everyone, [(i + 1, i) for i in range(count - 1)])  12.5 us
    all_to_all x1, starting transfers between devices, shards(): lax.all_to_all(slots, 'grp', split_axis=0, concat_axis=0, tiled=True)  5.97 us
    pallas_call x1, Pallas kernels, shards(): pl.pallas_call(functools.partial(coarse_kernel, layers), out_shape=jax.Sh...  4.63 us
    ppermute x1, starting transfers between devices, shards(): lax.ppermute(last, everyone, [(i, i + 1) for i in range(count - 1)])  4.28 us
    pallas_call x1, Pallas kernels, shards(): pl.pallas_call(functools.partial(spread_kernel, sizes, coarse.shape[0], c...  4.19 us
    pallas_call x1, Pallas kernels, shards(): pl.pallas_call(functools.partial(inner_kernel, layers), out_shape=[jax.Sh...  2.65 us
  transfers between devices with their start and end apart: 3, of which 1 were waited for; matrix products, arithmetic and copies ran while one was open for 0% of the time, Pallas kernels for 13%

profile of v4, /device:TPU:56, one launch (start us, length us, event | category | flops | bytes accessed | tf_op | source)
XLA Modules:
  0.0 88.2 jit_solution(12713762523878685916)
XLA Ops:
  0.6 1.6 %edge_layers.1 = (bf16[64,128]{1,0:T(8,128)(2,1)S(1)}, bf16[64,128]{1,0:T(8,128)(2,1)S(1)}, bf16[1024,160]{1,0:T(8,128)(2,1)S(1)}, bf16[1024,160]{1,0:T(8,128)(2,1)S(1)}) custom-call(bf16[1024,160]{1,0:T(8,128)(2,1)} %bitcast.15, bf16[1024,160]{1,0:T(8,128)(2,1)} %bitcast.16), custom_call_target="tpu_custom_call" | custom-call | flops 10000000 | bytes 1000000 | tf_op jit(solution)/shard_map/edge_layers/pallas_call | solution.py:308
  2.2 4.3 %collective-permute-start = (bf16[64,128]{1,0:T(8,128)(2,1)S(1)}, bf16[64,128]{1,0:T(8,128)(2,1)S(1)}, u32[]{:S(2)}, u32[]{:S(2)}) collective-permute-start(bf16[64,128]{1,0:T(8,128)(2,1)S(1)} %get-tuple-element.9), channel_id=1, source_target_pairs={{0,1},{1,2},{2,3},{3,4},{4,5},{5,6},{6,7},{7,8},{8,9},{9,10},{10,1... | collective-permute-start | bytes 49160 | tf_op jit(solution)/shard_map/ppermute | solution.py:320
  6.5 12.5 %collective-permute-start.1 = (bf16[64,128]{1,0:T(8,128)(2,1)S(1)}, bf16[64,128]{1,0:T(8,128)(2,1)S(1)}, u32[]{:S(2)}, u32[]{:S(2)}) collective-permute-start(bf16[64,128]{1,0:T(8,128)(2,1)S(1)} %get-tuple-element.10), channel_id=1, source_target_pairs={{1,0},{2,1},{3,2},{4,3},{5,4},{6,5},{7,6},{8,7},{9,8},{10,9},{11,1... | collective-permute-start | bytes 49160 | tf_op jit(solution)/shard_map/ppermute | solution.py:321
  19.0 2.6 %inner_layers.1 = (f32[160,128]{1,0:T(8,128)S(1)}, f32[1280,128]{1,0:T(8,128)S(1)}, bf16[12,512,128]{2,1,0:T(8,128)(2,1)}) custom-call(bf16[1024,160]{1,0:T(8,128)(2,1)S(1)} %get-tuple-element.11.f_in, bf16[1024,160]{1,0:T(8,128)(2,1)S(1)} %get-tuple-element.12.c_in), custom_call_target="tpu_custom_call" | custom-call | flops 100000000 | bytes 10000000 | tf_op jit(solution)/shard_map/inner_layers/pallas_call | solution.py:325
  21.6 0.0 collective-permute-done.before_ref
  21.6 0.0 collective-permute-done.1.after_ref
  21.6 1.6 %outer_layers.1 = bf16[12,512,128]{2,1,0:T(8,128)(2,1)} custom-call(s32[1,5]{1,0:T(1,128)} %bitcast.17, bf16[64,128]{1,0:T(8,128)(2,1)S(1)} %collective-permute-done.before_ref, bf16[64,128]{1,0:T(8,128)(2,1)S(1)} %collective-permute-done.1.after_ref, f32[160,128]{1,0:T(8,128)S(1)} %get-tuple-element.13.near_ref, ...), custom_call_target="tpu_custom_call", output_to_operand_aliasing={{}: (5, {})} | custom-call | tf_op jit(solution)/shard_map/outer_layers/pallas_call | solution.py:342
  23.2 6.0 %all-to-all-start = ((bf16[12,512,128]{2,1,0:T(8,128)(2,1)}), bf16[12,512,128]{2,1,0:T(8,128)(2,1)S(1)}, u32[]{:S(2)}, u32[]{:S(2)}) async-start(bf16[12,512,128]{2,1,0:T(8,128)(2,1)} %outer_layers.1), calls=%async_computation | async-start | bytes 3145728 | tf_op jit(solution)/shard_map/all_to_all | solution.py:379
  29.2 4.6 %coarse_rows.1 = f32[176,128]{1,0:T(8,128)S(1)} custom-call(bf16[64,128]{1,0:T(8,128)(2,1)S(1)} %collective-permute-done.before_ref, bf16[64,128]{1,0:T(8,128)(2,1)S(1)} %collective-permute-done.1.after_ref, bf16[1024,160]{1,0:T(8,128)(2,1)S(1)} %get-tuple-element.11.f_in, bf16[1024,160]{1,0:T(8,128)(2,1)S(1)} %get-tuple-element.12.c_in), custom_call_target="tpu_custom_call" | custom-call | flops 100000000 | bytes 10000000 | tf_op jit(solution)/shard_map/coarse_rows/pallas_call | solution.py:368
  33.9 12.7 %all_gather.6 = f16[704,128]{1,0:T(8,128)(2,1)S(1)} all-gather(f16[176,128]{1,0:T(8,128)(2,1)S(1)} %convert_element_type.6), channel_id=1, replica_groups=mesh['x'=4,'y'=8,'core'=2,'grp'=12] {'x'}, dimensions={0}, use_global_device_ids=true | all-gather | bytes 225280 | tf_op jit(solution)/shard_map/all_gather | solution.py:383
  46.5 23.3 %all-gather.1 = f16[11264,128]{1,0:T(8,128)(2,1)S(1)} all-gather(f16[704,128]{1,0:T(8,128)(2,1)S(1)} %all_gather.6), channel_id=1, replica_groups=mesh['x'=4,'y'=8,'core'=2,'grp'=12] {'y','core'}, dimensions={0}, use_global_device_ids=true | all-gather | bytes 3063808 | tf_op jit(solution)/shard_map/all_gather | solution.py:383
  69.8 0.4 convert_element_type.7.in_ref
  70.2 4.2 %spread_coarse.1 = f32[320,4096]{1,0:T(8,128)} custom-call(f32[11264,128]{1,0:T(8,128)S(1)} %convert_element_type.7.in_ref), custom_call_target="tpu_custom_call" | custom-call | tf_op jit(solution)/shard_map/spread_coarse/pallas_call | solution.py:386
  74.4 12.6 %all-to-all-done = bf16[12,512,128]{2,1,0:T(8,128)(2,1)S(1)} async-done(((bf16[12,512,128]{2,1,0:T(8,128)(2,1)}), bf16[12,512,128]{2,1,0:T(8,128)(2,1)S(1)}, u32[]{:S(2)}, u32[]{:S(2)}) %all-to-all-start) | async-done | bytes 1572896 | tf_op jit(solution)/shard_map/all_to_all | solution.py:379
  87.0 1.1 %copy.9 = bf16[1,1,12,2,32768]{4,3,2,1,0:T(2,128)(2,1)} copy(bf16[1,1,12,2,32768]{4,3,2,1,0:T(2,128)(2,1)S(1)} %bitcast.13) | data formatting | bytes 3145728
  (1 shorter events, 0.0 us)
Async XLA Ops:
  2.2 19.4 %collective-permute-start = (bf16[64,128]{1,0:T(8,128)(2,1)S(1)}, bf16[64,128]{1,0:T(8,128)(2,1)S(1)}, u32[]{:S(2)}, u32[]{:S(2)}) collective-permute-start(bf16[64,128]{1,0:T(8,128)(2,1)S(1)} %get-tuple-element.9), channel_id=1, source_target_pairs={{0,1},{1,2},{2,3},{3,4},{4,5},{5,6},{6,7},{7,8},{8,9},{9,10},{10,1... | collective-permute-start | bytes 49160 | tf_op jit(solution)/shard_map/ppermute | solution.py:320
  6.5 15.1 %collective-permute-start.1 = (bf16[64,128]{1,0:T(8,128)(2,1)S(1)}, bf16[64,128]{1,0:T(8,128)(2,1)S(1)}, u32[]{:S(2)}, u32[]{:S(2)}) collective-permute-start(bf16[64,128]{1,0:T(8,128)(2,1)S(1)} %get-tuple-element.10), channel_id=1, source_target_pairs={{1,0},{2,1},{3,2},{4,3},{5,4},{6,5},{7,6},{8,7},{9,8},{10,9},{11,1... | collective-permute-start | bytes 49160 | tf_op jit(solution)/shard_map/ppermute | solution.py:321
  23.2 63.8 %all-to-all-start = ((bf16[12,512,128]{2,1,0:T(8,128)(2,1)}), bf16[12,512,128]{2,1,0:T(8,128)(2,1)S(1)}, u32[]{:S(2)}, u32[]{:S(2)}) async-start(bf16[12,512,128]{2,1,0:T(8,128)(2,1)} %outer_layers.1), calls=%async_computation | async-start | bytes 3145728 | tf_op jit(solution)/shard_map/all_to_all | solution.py:379

commit v5 on v4

--- a/solution.py
+++ b/solution.py
@@ -10,7 +10,7 @@
 WEIGHT = 0.8
 F32, BF16, F16 = jnp.float32, jnp.bfloat16, jnp.float16
 HALO = 3
-STEP = 40
+STEP = 79
 EDGE = 2
 SIDE = 4
 SUB, LANES = 8, 128
@@ -137,7 +137,7 @@
         pairs = left.reshape(count // 2, 2, SUB, LANES)
         _store(pair_ref, (layer - lo) // 2 + pair_at, pairs[:, 0] + pairs[:, 1])
 
-    _chunks(lo, hi, STEP, body)
+    _chunks(lo, hi, 40, body)
 
 
 def _pooled(pair_ref, rows):

time: 88.4 us -> 88.4 us (level)
  no operation moved by 1% of the time
where the time goes in v5:
time: 88.4 us; the launch traced here: 88.2 us
  blocking collectives  35.9 us (41%)
  starting transfers between devices  22.9 us (26%)
  Pallas kernels  14.4 us (16%)
  waiting for transfers between devices  12.7 us (14%)
  local copies, waits for them, and re-layouts  1.14 us (1%)
    all_gather x2, blocking collectives, shards(): gathered = lax.all_gather(gathered, axes, axis=0, tiled=True)  35.9 us
    all_to_all x1, waiting for transfers between devices, shards(): lax.all_to_all(slots, 'grp', split_axis=0, concat_axis=0, tiled=True)  12.7 us
    ppermute x1, starting transfers between devices, shards(): lax.ppermute(first, everyone, [(i + 1, i) for i in range(count - 1)])  12.5 us
    all_to_all x1, starting transfers between devices, shards(): lax.all_to_all(slots, 'grp', split_axis=0, concat_axis=0, tiled=True)  6.19 us
    pallas_call x1, Pallas kernels, shards(): pl.pallas_call(functools.partial(coarse_kernel, layers), out_shape=jax.Sh...  4.57 us
    ppermute x1, starting transfers between devices, shards(): lax.ppermute(last, everyone, [(i, i + 1) for i in range(count - 1)])  4.28 us
    pallas_call x1, Pallas kernels, shards(): pl.pallas_call(functools.partial(spread_kernel, sizes, coarse.shape[0], c...  4.19 us
    pallas_call x1, Pallas kernels, shards(): pl.pallas_call(functools.partial(inner_kernel, layers), out_shape=[jax.Sh...  2.43 us
  transfers between devices with their start and end apart: 3, of which 1 were waited for; matrix products, arithmetic and copies ran while one was open for 0% of the time, Pallas kernels for 13%

profile of v5, /device:TPU:56, one launch (start us, length us, event | category | flops | bytes accessed | tf_op | source)
XLA Modules:
  0.0 88.2 jit_solution(8816091176925133627)
XLA Ops:
  0.6 1.6 %edge_layers.1 = (bf16[64,128]{1,0:T(8,128)(2,1)S(1)}, bf16[64,128]{1,0:T(8,128)(2,1)S(1)}, bf16[1024,160]{1,0:T(8,128)(2,1)S(1)}, bf16[1024,160]{1,0:T(8,128)(2,1)S(1)}) custom-call(bf16[1024,160]{1,0:T(8,128)(2,1)} %bitcast.15, bf16[1024,160]{1,0:T(8,128)(2,1)} %bitcast.16), custom_call_target="tpu_custom_call" | custom-call | flops 10000000 | bytes 1000000 | tf_op jit(solution)/shard_map/edge_layers/pallas_call | solution.py:308
  2.2 4.3 %collective-permute-start = (bf16[64,128]{1,0:T(8,128)(2,1)S(1)}, bf16[64,128]{1,0:T(8,128)(2,1)S(1)}, u32[]{:S(2)}, u32[]{:S(2)}) collective-permute-start(bf16[64,128]{1,0:T(8,128)(2,1)S(1)} %get-tuple-element.9), channel_id=1, source_target_pairs={{0,1},{1,2},{2,3},{3,4},{4,5},{5,6},{6,7},{7,8},{8,9},{9,10},{10,1... | collective-permute-start | bytes 49160 | tf_op jit(solution)/shard_map/ppermute | solution.py:320
  6.5 12.5 %collective-permute-start.1 = (bf16[64,128]{1,0:T(8,128)(2,1)S(1)}, bf16[64,128]{1,0:T(8,128)(2,1)S(1)}, u32[]{:S(2)}, u32[]{:S(2)}) collective-permute-start(bf16[64,128]{1,0:T(8,128)(2,1)S(1)} %get-tuple-element.10), channel_id=1, source_target_pairs={{1,0},{2,1},{3,2},{4,3},{5,4},{6,5},{7,6},{8,7},{9,8},{10,9},{11,1... | collective-permute-start | bytes 49160 | tf_op jit(solution)/shard_map/ppermute | solution.py:321
  19.0 2.4 %inner_layers.1 = (f32[160,128]{1,0:T(8,128)S(1)}, f32[1280,128]{1,0:T(8,128)S(1)}, bf16[12,512,128]{2,1,0:T(8,128)(2,1)}) custom-call(bf16[1024,160]{1,0:T(8,128)(2,1)S(1)} %get-tuple-element.11.f_in, bf16[1024,160]{1,0:T(8,128)(2,1)S(1)} %get-tuple-element.12.c_in), custom_call_target="tpu_custom_call" | custom-call | flops 100000000 | bytes 10000000 | tf_op jit(solution)/shard_map/inner_layers/pallas_call | solution.py:325
  21.4 0.0 collective-permute-done.before_ref
  21.4 0.0 collective-permute-done.1.after_ref
  21.4 1.6 %outer_layers.1 = bf16[12,512,128]{2,1,0:T(8,128)(2,1)} custom-call(s32[1,5]{1,0:T(1,128)} %bitcast.17, bf16[64,128]{1,0:T(8,128)(2,1)S(1)} %collective-permute-done.before_ref, bf16[64,128]{1,0:T(8,128)(2,1)S(1)} %collective-permute-done.1.after_ref, f32[160,128]{1,0:T(8,128)S(1)} %get-tuple-element.13.near_ref, ...), custom_call_target="tpu_custom_call", output_to_operand_aliasing={{}: (5, {})} | custom-call | tf_op jit(solution)/shard_map/outer_layers/pallas_call | solution.py:342
  23.0 6.2 %all-to-all-start = ((bf16[12,512,128]{2,1,0:T(8,128)(2,1)}), bf16[12,512,128]{2,1,0:T(8,128)(2,1)S(1)}, u32[]{:S(2)}, u32[]{:S(2)}) async-start(bf16[12,512,128]{2,1,0:T(8,128)(2,1)} %outer_layers.1), calls=%async_computation | async-start | bytes 3145728 | tf_op jit(solution)/shard_map/all_to_all | solution.py:379
  29.2 4.6 %coarse_rows.1 = f32[176,128]{1,0:T(8,128)S(1)} custom-call(bf16[64,128]{1,0:T(8,128)(2,1)S(1)} %collective-permute-done.before_ref, bf16[64,128]{1,0:T(8,128)(2,1)S(1)} %collective-permute-done.1.after_ref, bf16[1024,160]{1,0:T(8,128)(2,1)S(1)} %get-tuple-element.11.f_in, bf16[1024,160]{1,0:T(8,128)(2,1)S(1)} %get-tuple-element.12.c_in), custom_call_target="tpu_custom_call" | custom-call | flops 100000000 | bytes 10000000 | tf_op jit(solution)/shard_map/coarse_rows/pallas_call | solution.py:368
  33.8 12.7 %all_gather.6 = f16[704,128]{1,0:T(8,128)(2,1)S(1)} all-gather(f16[176,128]{1,0:T(8,128)(2,1)S(1)} %convert_element_type.6), channel_id=1, replica_groups=mesh['x'=4,'y'=8,'core'=2,'grp'=12] {'x'}, dimensions={0}, use_global_device_ids=true | all-gather | bytes 225280 | tf_op jit(solution)/shard_map/all_gather | solution.py:383
  46.5 23.2 %all-gather.1 = f16[11264,128]{1,0:T(8,128)(2,1)S(1)} all-gather(f16[704,128]{1,0:T(8,128)(2,1)S(1)} %all_gather.6), channel_id=1, replica_groups=mesh['x'=4,'y'=8,'core'=2,'grp'=12] {'y','core'}, dimensions={0}, use_global_device_ids=true | all-gather | bytes 3063808 | tf_op jit(solution)/shard_map/all_gather | solution.py:383
  69.7 0.4 convert_element_type.7.in_ref
  70.1 4.2 %spread_coarse.1 = f32[320,4096]{1,0:T(8,128)} custom-call(f32[11264,128]{1,0:T(8,128)S(1)} %convert_element_type.7.in_ref), custom_call_target="tpu_custom_call" | custom-call | tf_op jit(solution)/shard_map/spread_coarse/pallas_call | solution.py:386
  74.3 12.7 %all-to-all-done = bf16[12,512,128]{2,1,0:T(8,128)(2,1)S(1)} async-done(((bf16[12,512,128]{2,1,0:T(8,128)(2,1)}), bf16[12,512,128]{2,1,0:T(8,128)(2,1)S(1)}, u32[]{:S(2)}, u32[]{:S(2)}) %all-to-all-start) | async-done | bytes 1572896 | tf_op jit(solution)/shard_map/all_to_all | solution.py:379
  87.0 1.1 %copy.9 = bf16[1,1,12,2,32768]{4,3,2,1,0:T(2,128)(2,1)} copy(bf16[1,1,12,2,32768]{4,3,2,1,0:T(2,128)(2,1)S(1)} %bitcast.13) | data formatting | bytes 3145728
  (1 shorter events, 0.0 us)
Async XLA Ops:
  2.2 19.2 %collective-permute-start = (bf16[64,128]{1,0:T(8,128)(2,1)S(1)}, bf16[64,128]{1,0:T(8,128)(2,1)S(1)}, u32[]{:S(2)}, u32[]{:S(2)}) collective-permute-start(bf16[64,128]{1,0:T(8,128)(2,1)S(1)} %get-tuple-element.9), channel_id=1, source_target_pairs={{0,1},{1,2},{2,3},{3,4},{4,5},{5,6},{6,7},{7,8},{8,9},{9,10},{10,1... | collective-permute-start | bytes 49160 | tf_op jit(solution)/shard_map/ppermute | solution.py:320
  6.5 14.9 %collective-permute-start.1 = (bf16[64,128]{1,0:T(8,128)(2,1)S(1)}, bf16[64,128]{1,0:T(8,128)(2,1)S(1)}, u32[]{:S(2)}, u32[]{:S(2)}) collective-permute-start(bf16[64,128]{1,0:T(8,128)(2,1)S(1)} %get-tuple-element.10), channel_id=1, source_target_pairs={{1,0},{2,1},{3,2},{4,3},{5,4},{6,5},{7,6},{8,7},{9,8},{10,9},{11,1... | collective-permute-start | bytes 49160 | tf_op jit(solution)/shard_map/ppermute | solution.py:321
  23.0 64.0 %all-to-all-start = ((bf16[12,512,128]{2,1,0:T(8,128)(2,1)}), bf16[12,512,128]{2,1,0:T(8,128)(2,1)S(1)}, u32[]{:S(2)}, u32[]{:S(2)}) async-start(bf16[12,512,128]{2,1,0:T(8,128)(2,1)} %outer_layers.1), calls=%async_computation | async-start | bytes 3145728 | tf_op jit(solution)/shard_map/all_to_all | solution.py:379

commit v6 on v4

--- a/solution.py
+++ b/solution.py
@@ -201,7 +201,7 @@
 
 def outer_kernel(layers, box_rows, boxes, owner_in, before_ref, after_ref, near_ref, u2_in, slots_in, slots_ref, c_ref, f_ref, *work):
     del slots_in
-    *g, gz, w, u1, u2, settled_ref, mixed_ref, staged_ref, owner_ref, owner_sem, sems = work
+    *g, gz, w, u1, u2, mixed_ref, staged_ref, owner_ref, owner_sem, sems = work
     load = pltpu.make_async_copy(owner_in, owner_ref, owner_sem.at[0])
     load.start()
     span = EDGE + 2 * HALO
@@ -213,11 +213,9 @@
         ref[span * SUB : total * SUB - halo, :] = near_ref[(2 * at + 1) * own : (2 * at + 2) * own, :]
         ref[total * SUB - halo :, :] = _halo(after_ref, at, False)
     _sweeps(c_ref, f_ref, g, gz, w, u1, u2, None, HALO, total - HALO, True)
-    rows = layers * SUB
     edge = EDGE * SUB
-    settled_ref[edge : rows - edge, :] = u2_in[edge : rows - edge, :]
-    settled_ref[:edge, :] = u2[halo : halo + edge, :]
-    settled_ref[rows - edge :, :] = u2[span * SUB + halo : span * SUB + halo + edge, :]
+    late = 2 * (box_rows - edge)
+    head, tail = u2[halo : halo + edge, :], u2[span * SUB + halo : span * SUB + halo + edge, :]
     load.wait()
 
     owners = [owner_ref[0, k] for k in range(boxes)]
@@ -232,10 +230,18 @@
 
         @pl.when(first == k)
         def _():
-            mixed_ref[pl.ds(0, box_rows, stride=2), :] = settled_ref[k * box_rows : (k + 1) * box_rows, :]
+            mixed_ref[pl.ds(0, box_rows, stride=2), :] = u2_in[k * box_rows : (k + 1) * box_rows, :]
             start = pl.multiple_of(jnp.maximum(second, 0) * box_rows, box_rows)
-            cells = settled_ref[pl.ds(start, box_rows), :]
-            mixed_ref[pl.ds(1, box_rows, stride=2), :] = jnp.where(second >= 0, cells, 0.0)
+            mixed_ref[pl.ds(1, box_rows, stride=2), :] = jnp.where(second >= 0, u2_in[pl.ds(start, box_rows), :], 0.0)
+            if k == 0:
+                mixed_ref[pl.ds(0, edge, stride=2), :] = head
+            if k == boxes - 1:
+                mixed_ref[pl.ds(late, edge, stride=2), :] = tail
+
+            @pl.when(second == boxes - 1)
+            def _():
+                mixed_ref[pl.ds(late + 1, edge, stride=2), :] = tail
+
             staged_ref[k] = mixed_ref[...].astype(BF16)
 
         sends.append(pltpu.make_async_copy(staged_ref.at[first], slots_ref.at[owners[k]], sems.at[k]))
@@ -345,7 +351,6 @@
         in_specs=[hbm] + _whole(4) + [hbm],
         out_specs=hbm,
         scratch_shapes=_scratch(total, 10)
-        + _scratch(layers, 1)
         + _scratch(2 * depth, 1)
         + [
             pltpu.VMEM((boxes,) + slots_shape[1:], BF16),

time: 88.4 us -> 88.5 us (level)
  no operation moved by 1% of the time
where the time goes in v6:
time: 88.5 us; the launch traced here: 88.3 us
  blocking collectives  35.9 us (41%)
  starting transfers between devices  22.7 us (26%)
  Pallas kernels  14.7 us (17%)
  waiting for transfers between devices  12.6 us (14%)
  local copies, waits for them, and re-layouts  1.14 us (1%)
    all_gather x2, blocking collectives, shards(): gathered = lax.all_gather(gathered, axes, axis=0, tiled=True)  35.9 us
    all_to_all x1, waiting for transfers between devices, shards(): lax.all_to_all(slots, 'grp', split_axis=0, concat_axis=0, tiled=True)  12.6 us
    ppermute x1, starting transfers between devices, shards(): lax.ppermute(first, everyone, [(i + 1, i) for i in range(count - 1)])  12.5 us
    all_to_all x1, starting transfers between devices, shards(): lax.all_to_all(slots, 'grp', split_axis=0, concat_axis=0, tiled=True)  5.98 us
    pallas_call x1, Pallas kernels, shards(): pl.pallas_call(functools.partial(coarse_kernel, layers), out_shape=jax.Sh...  4.62 us
    ppermute x1, starting transfers between devices, shards(): lax.ppermute(last, everyone, [(i, i + 1) for i in range(count - 1)])  4.28 us
    pallas_call x1, Pallas kernels, shards(): pl.pallas_call(functools.partial(spread_kernel, sizes, coarse.shape[0], c...  4.19 us
    pallas_call x1, Pallas kernels, shards(): pl.pallas_call(functools.partial(inner_kernel, layers), out_shape=[jax.Sh...  2.65 us
  transfers between devices with their start and end apart: 3, of which 1 were waited for; matrix products, arithmetic and copies ran while one was open for 0% of the time, Pallas kernels for 13%

profile of v6, /device:TPU:56, one launch (start us, length us, event | category | flops | bytes accessed | tf_op | source)
XLA Modules:
  0.0 88.3 jit_solution(4149598176362490864)
XLA Ops:
  0.6 1.6 %edge_layers.1 = (bf16[64,128]{1,0:T(8,128)(2,1)S(1)}, bf16[64,128]{1,0:T(8,128)(2,1)S(1)}, bf16[1024,160]{1,0:T(8,128)(2,1)S(1)}, bf16[1024,160]{1,0:T(8,128)(2,1)S(1)}) custom-call(bf16[1024,160]{1,0:T(8,128)(2,1)} %bitcast.15, bf16[1024,160]{1,0:T(8,128)(2,1)} %bitcast.16), custom_call_target="tpu_custom_call" | custom-call | flops 10000000 | bytes 1000000 | tf_op jit(solution)/shard_map/edge_layers/pallas_call | solution.py:314
  2.2 4.3 %collective-permute-start = (bf16[64,128]{1,0:T(8,128)(2,1)S(1)}, bf16[64,128]{1,0:T(8,128)(2,1)S(1)}, u32[]{:S(2)}, u32[]{:S(2)}) collective-permute-start(bf16[64,128]{1,0:T(8,128)(2,1)S(1)} %get-tuple-element.9), channel_id=1, source_target_pairs={{0,1},{1,2},{2,3},{3,4},{4,5},{5,6},{6,7},{7,8},{8,9},{9,10},{10,1... | collective-permute-start | bytes 49160 | tf_op jit(solution)/shard_map/ppermute | solution.py:326
  6.5 12.5 %collective-permute-start.1 = (bf16[64,128]{1,0:T(8,128)(2,1)S(1)}, bf16[64,128]{1,0:T(8,128)(2,1)S(1)}, u32[]{:S(2)}, u32[]{:S(2)}) collective-permute-start(bf16[64,128]{1,0:T(8,128)(2,1)S(1)} %get-tuple-element.10), channel_id=1, source_target_pairs={{1,0},{2,1},{3,2},{4,3},{5,4},{6,5},{7,6},{8,7},{9,8},{10,9},{11,1... | collective-permute-start | bytes 49160 | tf_op jit(solution)/shard_map/ppermute | solution.py:327
  19.0 2.6 %inner_layers.1 = (f32[160,128]{1,0:T(8,128)S(1)}, f32[1280,128]{1,0:T(8,128)S(1)}, bf16[12,512,128]{2,1,0:T(8,128)(2,1)}) custom-call(bf16[1024,160]{1,0:T(8,128)(2,1)S(1)} %get-tuple-element.11.f_in, bf16[1024,160]{1,0:T(8,128)(2,1)S(1)} %get-tuple-element.12.c_in), custom_call_target="tpu_custom_call" | custom-call | flops 100000000 | bytes 10000000 | tf_op jit(solution)/shard_map/inner_layers/pallas_call | solution.py:331
  21.6 0.0 collective-permute-done.before_ref
  21.6 0.0 collective-permute-done.1.after_ref
  21.6 1.7 %outer_layers.1 = bf16[12,512,128]{2,1,0:T(8,128)(2,1)} custom-call(s32[1,5]{1,0:T(1,128)} %bitcast.17, bf16[64,128]{1,0:T(8,128)(2,1)S(1)} %collective-permute-done.before_ref, bf16[64,128]{1,0:T(8,128)(2,1)S(1)} %collective-permute-done.1.after_ref, f32[160,128]{1,0:T(8,128)S(1)} %get-tuple-element.13.near_ref, ...), custom_call_target="tpu_custom_call", output_to_operand_aliasing={{}: (5, {})} | custom-call | tf_op jit(solution)/shard_map/outer_layers/pallas_call | solution.py:348
  23.3 6.0 %all-to-all-start = ((bf16[12,512,128]{2,1,0:T(8,128)(2,1)}), bf16[12,512,128]{2,1,0:T(8,128)(2,1)S(1)}, u32[]{:S(2)}, u32[]{:S(2)}) async-start(bf16[12,512,128]{2,1,0:T(8,128)(2,1)} %outer_layers.1), calls=%async_computation | async-start | bytes 3145728 | tf_op jit(solution)/shard_map/all_to_all | solution.py:384
  29.3 4.6 %coarse_rows.1 = f32[176,128]{1,0:T(8,128)S(1)} custom-call(bf16[64,128]{1,0:T(8,128)(2,1)S(1)} %collective-permute-done.before_ref, bf16[64,128]{1,0:T(8,128)(2,1)S(1)} %collective-permute-done.1.after_ref, bf16[1024,160]{1,0:T(8,128)(2,1)S(1)} %get-tuple-element.11.f_in, bf16[1024,160]{1,0:T(8,128)(2,1)S(1)} %get-tuple-element.12.c_in), custom_call_target="tpu_custom_call" | custom-call | flops 100000000 | bytes 10000000 | tf_op jit(solution)/shard_map/coarse_rows/pallas_call | solution.py:373
  34.0 12.7 %all_gather.6 = f16[704,128]{1,0:T(8,128)(2,1)S(1)} all-gather(f16[176,128]{1,0:T(8,128)(2,1)S(1)} %convert_element_type.6), channel_id=1, replica_groups=mesh['x'=4,'y'=8,'core'=2,'grp'=12] {'x'}, dimensions={0}, use_global_device_ids=true | all-gather | bytes 225280 | tf_op jit(solution)/shard_map/all_gather | solution.py:388
  46.6 23.3 %all-gather.1 = f16[11264,128]{1,0:T(8,128)(2,1)S(1)} all-gather(f16[704,128]{1,0:T(8,128)(2,1)S(1)} %all_gather.6), channel_id=1, replica_groups=mesh['x'=4,'y'=8,'core'=2,'grp'=12] {'y','core'}, dimensions={0}, use_global_device_ids=true | all-gather | bytes 3063808 | tf_op jit(solution)/shard_map/all_gather | solution.py:388
  69.9 0.4 convert_element_type.7.in_ref
  70.3 4.2 %spread_coarse.1 = f32[320,4096]{1,0:T(8,128)} custom-call(f32[11264,128]{1,0:T(8,128)S(1)} %convert_element_type.7.in_ref), custom_call_target="tpu_custom_call" | custom-call | tf_op jit(solution)/shard_map/spread_coarse/pallas_call | solution.py:391
  74.5 12.6 %all-to-all-done = bf16[12,512,128]{2,1,0:T(8,128)(2,1)S(1)} async-done(((bf16[12,512,128]{2,1,0:T(8,128)(2,1)}), bf16[12,512,128]{2,1,0:T(8,128)(2,1)S(1)}, u32[]{:S(2)}, u32[]{:S(2)}) %all-to-all-start) | async-done | bytes 1572896 | tf_op jit(solution)/shard_map/all_to_all | solution.py:384
  87.1 1.1 %copy.9 = bf16[1,1,12,2,32768]{4,3,2,1,0:T(2,128)(2,1)} copy(bf16[1,1,12,2,32768]{4,3,2,1,0:T(2,128)(2,1)S(1)} %bitcast.13) | data formatting | bytes 3145728
  (1 shorter events, 0.0 us)
Async XLA Ops:
  2.2 19.4 %collective-permute-start = (bf16[64,128]{1,0:T(8,128)(2,1)S(1)}, bf16[64,128]{1,0:T(8,128)(2,1)S(1)}, u32[]{:S(2)}, u32[]{:S(2)}) collective-permute-start(bf16[64,128]{1,0:T(8,128)(2,1)S(1)} %get-tuple-element.9), channel_id=1, source_target_pairs={{0,1},{1,2},{2,3},{3,4},{4,5},{5,6},{6,7},{7,8},{8,9},{9,10},{10,1... | collective-permute-start | bytes 49160 | tf_op jit(solution)/shard_map/ppermute | solution.py:326
  6.5 15.1 %collective-permute-start.1 = (bf16[64,128]{1,0:T(8,128)(2,1)S(1)}, bf16[64,128]{1,0:T(8,128)(2,1)S(1)}, u32[]{:S(2)}, u32[]{:S(2)}) collective-permute-start(bf16[64,128]{1,0:T(8,128)(2,1)S(1)} %get-tuple-element.10), channel_id=1, source_target_pairs={{1,0},{2,1},{3,2},{4,3},{5,4},{6,5},{7,6},{8,7},{9,8},{10,9},{11,1... | collective-permute-start | bytes 49160 | tf_op jit(solution)/shard_map/ppermute | solution.py:327
  23.3 63.8 %all-to-all-start = ((bf16[12,512,128]{2,1,0:T(8,128)(2,1)}), bf16[12,512,128]{2,1,0:T(8,128)(2,1)S(1)}, u32[]{:S(2)}, u32[]{:S(2)}) async-start(bf16[12,512,128]{2,1,0:T(8,128)(2,1)} %outer_layers.1), calls=%async_computation | async-start | bytes 3145728 | tf_op jit(solution)/shard_map/all_to_all | solution.py:384
